TPU v7x, 256 devices: a whole 4x4x8 slice. The times are simulated.
256 devices in a mesh: row: 16 (over z, x_hi), col: 16 (over y, x_lo, core).
Axes of the slice: x: 4 (x_hi: 2, x_lo: 2; x = x_hi * 2 + x_lo), y: 4, z: 8, core: 2. Of those that a mesh axis runs over, the one named last changes fastest.
Arguments:
- query_rows: bfloat16 [128, 256, 2048], P('row', 'col'), may hold values from -6 to 6
- key_rows: bfloat16 [128, 256, 2048], P('row', 'col'), may hold values from -6 to 6
- value_rows: bfloat16 [128, 256, 2048], P('row', 'col'), may hold values from -6 to 6
- grad_out: bfloat16 [128, 256, 2048], P('row', 'col'), may hold values from -48 to 48
- log_norm: float32 [128, 256, 16], P('row', 'col'), may hold values from 5.5 to 7.5
- grad_offset: float32 [128, 256, 16], P('row', 'col'), may hold values from -192 to 192
- listed: int32 [256, 64], P(('row', 'col')), may hold values from 0 to 255, all different within a row
Outputs:
- grad_query: float32 [128, 256, 2048], P('row', 'col')
- grad_key: float32 [128, 256, 2048], P('row', 'col')
- grad_value: float32 [128, 256, 2048], P('row', 'col')
Inputs may be any that keep to these rules, and one draw needn't show every extreme that they name: Each query block lists 64 different summary blocks; every block is listed by some query block.
All inputs are finite; a program needn't handle non-finite values.
Results may differ from a plain program's by a relative error of at most 0.0034.
Values may be sent and summed in bfloat16 or wider, within the bound.
A program may use at most 128 MiB of HBM per device.

v0:
```python
import math

import jax
import jax.numpy as jnp
from jax import lax
from jax.sharding import PartitionSpec as P


def with_halo(block, sides, width):
    for axis, dim in sides:
        count = lax.axis_size(axis)
        forward = [(i, i + 1) for i in range(count - 1)]
        backward = [(target, source) for source, target in forward]
        low = lax.ppermute(
            lax.slice_in_dim(block, block.shape[dim] - width, None, axis=dim), axis, forward
        )
        high = lax.ppermute(lax.slice_in_dim(block, 0, width, axis=dim), axis, backward)
        block = jnp.concatenate([low, block, high], axis=dim)
    return block


def from_behind(value, axis, steps):
    count = lax.axis_size(axis)
    first, last = (max(0, -steps), min(count, count - steps))
    return lax.ppermute(value, axis, [(source, source + steps) for source in range(first, last)])


def grid_coords(first_row, first_column, count_rows, count_columns):
    row_index = first_row + jnp.arange(count_rows, dtype=jnp.int32)
    column_index = first_column + jnp.arange(count_columns, dtype=jnp.int32)
    return (
        jnp.broadcast_to(row_index[:, None], (count_rows, count_columns)).reshape(-1),
        jnp.broadcast_to(column_index[None, :], (count_rows, count_columns)).reshape(-1),
    )


def window_mask(query_at, target_at, radius, limits):
    nearby = (jnp.abs(query_at[0][:, None] - target_at[0][None, :]) <= radius) & (
        jnp.abs(query_at[1][:, None] - target_at[1][None, :]) <= radius
    )
    query_inside = (
        (query_at[0] >= 0)
        & (query_at[0] < limits[0])
        & (query_at[1] >= 0)
        & (query_at[1] < limits[1])
    )
    target_inside = (
        (target_at[0] >= 0)
        & (target_at[0] < limits[0])
        & (target_at[1] >= 0)
        & (target_at[1] < limits[1])
    )
    return nearby & query_inside[:, None] & target_inside[None, :]


def group_grads(query_part, grad_part, norm_part, offset_part, key_part, value_part, allowed):
    query_count = query_part.shape[0]
    key_count = key_part.shape[0]
    group_heads = norm_part.shape[1]
    head_size = query_part.shape[1] // group_heads
    score_scale = 1.0 / math.sqrt(head_size)
    query_three = query_part.reshape(query_count, group_heads, head_size)
    grad_three = grad_part.reshape(query_count, group_heads, head_size)
    key_three = key_part.reshape(key_count, group_heads, head_size)
    value_three = value_part.reshape(key_count, group_heads, head_size)
    scores = (
        jnp.einsum("qhd,khd->hqk", query_three, key_three, preferred_element_type=jnp.float32)
        * score_scale
    )
    weights = jnp.where(allowed[None], jnp.exp(scores - norm_part.T[:, :, None]), jnp.float32(0.0))
    grad_weights = jnp.einsum(
        "qhd,khd->hqk", grad_three, value_three, preferred_element_type=jnp.float32
    )
    grad_scores = weights * (grad_weights - offset_part.T[:, :, None]) * score_scale
    grad_low = grad_scores.astype(jnp.bfloat16)
    weights_low = weights.astype(jnp.bfloat16)
    grad_key = jnp.einsum(
        "hqk,qhd->khd", grad_low, query_three, preferred_element_type=jnp.float32
    ).reshape(key_count, -1)
    grad_value = jnp.einsum(
        "hqk,qhd->khd", weights_low, grad_three, preferred_element_type=jnp.float32
    ).reshape(key_count, -1)
    grad_query = jnp.einsum(
        "hqk,khd->qhd", grad_low, key_three, preferred_element_type=jnp.float32
    ).reshape(query_count, -1)
    return (grad_query, grad_key, grad_value)


def pair_grads(query_part, grad_part, norm_part, offset_part, key_part, value_part, allowed):
    head_count = norm_part.shape[1]
    per_group = math.gcd(head_count, 4)
    groups = head_count // per_group

    def split_heads(source):
        return jnp.moveaxis(source.reshape(source.shape[0], groups, -1), 1, 0)

    def run_group(pieces):
        return group_grads(
            pieces[0], pieces[1], pieces[2], pieces[3], pieces[4], pieces[5], allowed
        )

    results = lax.map(
        run_group,
        (
            split_heads(query_part),
            split_heads(grad_part),
            split_heads(norm_part),
            split_heads(offset_part),
            split_heads(key_part),
            split_heads(value_part),
        ),
    )
    return tuple((jnp.moveaxis(result, 0, 1).reshape(result.shape[1], -1) for result in results))


def on_device(query_rows, key_rows, value_rows, grad_out, log_norm, grad_offset, listed):
    tile_rows, tile_columns, features = query_rows.shape
    head_count = log_norm.shape[2]
    radius = tile_columns // 2
    tokens = tile_rows * tile_columns
    row_count = lax.axis_size("row")
    column_count = lax.axis_size("col")
    blocks = row_count * column_count
    limits = (tile_rows * row_count, tile_columns * column_count)
    row_start = lax.axis_index("row") * tile_rows
    column_start = lax.axis_index("col") * tile_columns
    pool_scale = 1.0 / math.sqrt(tokens)
    window_rows = tile_rows + 2 * radius
    window_columns = tile_columns + 2 * radius
    query_flat = query_rows.reshape(tokens, features)
    grad_flat = grad_out.reshape(tokens, features)
    norm_flat = log_norm.reshape(tokens, head_count)
    offset_flat = grad_offset.reshape(tokens, head_count)
    summary = jnp.stack(
        [
            jnp.sum(key_rows, axis=(0, 1), dtype=jnp.float32),
            jnp.sum(value_rows, axis=(0, 1), dtype=jnp.float32),
        ]
    )
    summary = (summary * pool_scale).astype(jnp.bfloat16)[None]
    summary_table = lax.all_gather(summary, ("row", "col"), axis=0, tiled=True)
    chosen = listed[0]
    picked = jnp.take(summary_table, chosen, axis=0)
    summary_query, summary_key, summary_value = pair_grads(
        query_flat,
        grad_flat,
        norm_flat,
        offset_flat,
        picked[:, 0],
        picked[:, 1],
        jnp.ones((tokens, picked.shape[0]), jnp.bool_),
    )
    stacked = jnp.stack([key_rows, value_rows], axis=2)
    extended = with_halo(stacked, (("row", 0), ("col", 1)), radius)
    key_window = extended[:, :, 0].reshape(-1, features)
    value_window = extended[:, :, 1].reshape(-1, features)
    own_at = grid_coords(row_start, column_start, tile_rows, tile_columns)
    window_at = grid_coords(row_start - radius, column_start - radius, window_rows, window_columns)
    allowed = window_mask(own_at, window_at, radius, limits)
    window_query, key_part, value_part = pair_grads(
        query_flat, grad_flat, norm_flat, offset_flat, key_window, value_window, allowed
    )
    shape_window = (window_rows, window_columns, features)
    gradient_rims = jnp.stack(
        [key_part.reshape(shape_window), value_part.reshape(shape_window)], axis=2
    )
    upper_rim = gradient_rims[:radius]
    lower_rim = gradient_rims[tile_rows + radius :]
    from_below = from_behind(upper_rim, "row", -1)
    from_above = from_behind(lower_rim, "row", 1)
    middle_band = gradient_rims[radius : tile_rows + radius]
    middle_band = middle_band.at[:radius].add(from_above).at[tile_rows - radius :].add(from_below)
    left_rim = middle_band[:, :radius]
    right_rim = middle_band[:, tile_columns + radius :]
    from_right = from_behind(left_rim, "col", -1)
    from_left = from_behind(right_rim, "col", 1)
    own_block = middle_band[:, radius : tile_columns + radius]
    own_block = (
        own_block.at[:, :radius].add(from_left).at[:, tile_columns - radius :].add(from_right)
    )
    window_key = own_block[:, :, 0]
    window_value = own_block[:, :, 1]
    selected = jnp.concatenate([summary_key, summary_value], axis=1)
    one_hot = (chosen[:, None] == jnp.arange(blocks, dtype=jnp.int32)[None, :]).astype(jnp.float32)
    spread_table = jnp.dot(one_hot.T, selected, precision=lax.Precision.HIGHEST)
    own_grad = lax.psum_scatter(
        spread_table, ("row", "col"), scatter_dimension=0, tiled=True
    ).reshape(-1)
    grad_query = (window_query + summary_query).reshape(tile_rows, tile_columns, features)
    grad_key = window_key + own_grad[:features] * pool_scale
    grad_value = window_value + own_grad[features:] * pool_scale
    return (grad_query, grad_key, grad_value)


def solution(mesh):
    in_specs = (
        P("row", "col", None),
        P("row", "col", None),
        P("row", "col", None),
        P("row", "col", None),
        P("row", "col", None),
        P("row", "col", None),
        P(("row", "col"), None),
    )
    out_specs = (P("row", "col", None), P("row", "col", None), P("row", "col", None))
    return jax.shard_map(
        on_device, mesh=mesh, in_specs=in_specs, out_specs=out_specs, check_vma=False
    )
```

profile of v0, /device:TPU:1, one launch (start us, length us, event | category | flops | bytes accessed | tf_op | source)
XLA Modules:
  0.0 968.4 jit_solution(7096832400056343471)
XLA Ops:
  9.8 6.2 collective-permute-start
  18.3 16.3 %collective-permute-done.1 = bf16[8,16,2,2048]{3,1,0,2:T(8,128)(2,1)S(1)} collective-permute-done((bf16[8,16,2,2048]{3,1,0,2:T(8,128)(2,1)S(1)}, bf16[8,16,2,2048]{3,1,0,2:T(8,128)(2,1)S(1)}, u32[]{:S(2)}, u32[]{:S(2)}) %collective-permute-start.1) | collective-permute-done | bytes 1048608 | tf_op jit(solution)/shard_map/ppermute | solution.py:17
  34.5 25.7 %collective-permute-done = bf16[8,16,2,2048]{3,1,0,2:T(8,128)(2,1)S(1)} collective-permute-done((bf16[8,16,2,2048]{3,1,0,2:T(8,128)(2,1)S(1)}, bf16[8,16,2,2048]{3,1,0,2:T(8,128)(2,1)S(1)}, u32[]{:S(2)}, u32[]{:S(2)}) %collective-permute-start) | collective-permute-done | bytes 1048608 | tf_op jit(solution)/shard_map/ppermute | solution.py:14
  79.8 20.3 %collective-permute-done.3 = bf16[24,8,2,2048]{3,1,0,2:T(8,128)(2,1)} collective-permute-done((bf16[24,8,2,2048]{3,1,0,2:T(8,128)(2,1)}, bf16[24,8,2,2048]{3,1,0,2:T(8,128)(2,1)}, u32[]{:S(2)}, u32[]{:S(2)}) %collective-permute-start.3) | collective-permute-done | bytes 1572896 | tf_op jit(solution)/shard_map/ppermute | solution.py:17
  105.8 3.9 reshape_reshape_squeeze.6
  109.7 4.4 copy.89
  114.1 6.1 reshape_reshape_squeeze.7
  120.3 6.0 copy.92
  127.3 32.7 %while.36 = (s32[]{:T(128)}, f32[4,128,512]{1,2,0:T(8,128)}, f32[4,768,512]{1,2,0:T(8,128)}, f32[4,768,512]{1,2,0:T(8,128)}, bf16[4,768,512]{1,2,0:T(8,128)(2,1)...) while((s32[]{:T(128)}, f32[4,128,512]{1,2,0:T(8,128)}, ...), condition=%wide.region_1.0_spmd.clone, body=%wide.region_0.0_spmd.clone.sunk | while | flops 507346944 | bytes 24072260 | solution.py:102
  159.9 7.8 copy.98
  167.8 8.5 stack_reshape_reshape.6
  176.3 7.8 copy.99
  184.1 8.5 stack_reshape_reshape.7
  192.6 3.4 constant_dynamic-update-slice_fusion.7
  197.6 4.2 fusion.34
  201.8 3.4 copy-done
  206.6 7.7 collective-permute-start.4
  214.3 436.9 %all-gather.2.cloned.1.call-done = bf16[256,2,2048]{2,1,0:T(2,128)(2,1)} async-done(((bf16[1,2,2048]{2,1,0:T(2,128)(2,1)}), bf16[256,2,2048]{2,1,0:T(2,128)(2,1)}) %all-gather.2.cloned.1.call-update) | async-done | bytes 2097168 | tf_op jit(solution)/shard_map/all_gather | solution.py:141
  651.2 3.2 gather_fusion
  657.7 13.4 %while.35 = (s32[]{:T(128)}, f32[4,128,512]{1,2,0:T(8,128)S(1)}, f32[4,64,512]{2,1,0:T(8,128)S(1)}, f32[4,64,512]{2,1,0:T(8,128)S(1)}, bf16[4,64,512]{2,1,0:T(8,...) while((s32[]{:T(128)}, f32[4,128,512]{1,2,0:T(8,128)S(1)}, ...), condition=%wide.region_5.6_spmd, body=%wide.region_4.5_spmd.sunk | while | flops 42172416 | bytes 4993173 | solution.py:102
  671.2 4.0 fusion.26
  675.2 6.0 fusion.21
  684.6 7.4 collective-permute-start.6
  698.6 256.3 %all-reduce.3.cloned.1.call-done = f32[256,4096]{1,0:T(8,128)} async-done(((f32[256,4096]{1,0:T(8,128)}), f32[256,4096]{1,0:T(8,128)}) %all-reduce.3.cloned.1.call-update) | async-done | bytes 4194320
  (227 shorter events, 99.3 us)
Async XLA Ops:
  7.2 644.0 %all-gather.2.cloned.1.call-start = ((), (), s32[]{:S(2)}) async-start(), calls=%async_computation | async-start | bytes 2105344 | tf_op jit(solution)/shard_map/all_gather | solution.py:141
  8.5 26.0 %collective-permute-start.1 = (bf16[8,16,2,2048]{3,1,0,2:T(8,128)(2,1)S(1)}, bf16[8,16,2,2048]{3,1,0,2:T(8,128)(2,1)S(1)}, u32[]{:S(2)}, u32[]{:S(2)}) collective-permute-start(bf16[8,16,2,2048]{3,1,0,2:T(8,128)(2,1)S(1)} %pad_maximum_fusion.2), channel_id=1, source_target_pairs={{16,0},{32,16},{48,32},{64,48},{80,64},{96,80},{112,96},{128,112},... | collective-permute-start | bytes 3145736 | tf_op jit(solution)/shard_map/ppermute | solution.py:17
  9.8 50.4 %collective-permute-start = (bf16[8,16,2,2048]{3,1,0,2:T(8,128)(2,1)S(1)}, bf16[8,16,2,2048]{3,1,0,2:T(8,128)(2,1)S(1)}, u32[]{:S(2)}, u32[]{:S(2)}) collective-permute-start(bf16[8,16,2,2048]{3,1,0,2:T(8,128)(2,1)S(1)} %pad_maximum_fusion.2), channel_id=1, source_target_pairs={{0,16},{16,32},{32,48},{48,64},{64,80},{80,96},{96,112},{112,128},... | collective-permute-start | bytes 3145736 | tf_op jit(solution)/shard_map/ppermute | solution.py:14
  61.6 12.8 %copy-start.9 = (f32[8,16,16]{2,1,0:T(8,128)S(1)}, f32[8,16,16]{2,1,0:T(8,128)}, u32[]{:S(2)}) copy-start(f32[8,16,16]{2,1,0:T(8,128)} %param.27) | copy-start | bytes 24580
  61.7 17.4 %copy-start.10 = (f32[8,16,16]{2,1,0:T(8,128)S(1)}, f32[8,16,16]{2,1,0:T(8,128)}, u32[]{:S(2)}) copy-start(f32[8,16,16]{2,1,0:T(8,128)} %param.28) | copy-start | bytes 24580
  61.7 18.1 %copy-start.11 = (s32[1,64]{1,0:T(1,128)S(1)}, s32[1,64]{1,0:T(1,128)}, u32[]{:S(2)}) copy-start(s32[1,64]{1,0:T(1,128)} %param.29) | copy-start | bytes 772
  61.7 38.4 %copy-start.4 = (bf16[8,16,2048]{2,1,0:T(8,128)(2,1)S(1)}, bf16[8,16,2048]{2,1,0:T(8,128)(2,1)}, u32[]{:S(2)}) copy-start(bf16[8,16,2048]{2,1,0:T(8,128)(2,1)} %param.25) | copy-start | bytes 1572868
  61.7 38.4 %copy-start.5 = (bf16[8,16,2048]{2,1,0:T(8,128)(2,1)S(1)}, bf16[8,16,2048]{2,1,0:T(8,128)(2,1)}, u32[]{:S(2)}) copy-start(bf16[8,16,2048]{2,1,0:T(8,128)(2,1)} %param.24) | copy-start | bytes 1572868
  63.7 36.4 %collective-permute-start.3 = (bf16[24,8,2,2048]{3,1,0,2:T(8,128)(2,1)}, bf16[24,8,2,2048]{3,1,0,2:T(8,128)(2,1)}, u32[]{:S(2)}, u32[]{:S(2)}) collective-permute-start(bf16[24,8,2,2048]{3,1,0,2:T(8,128)(2,1)} %get-tuple-element.371), channel_id=1, source_target_pairs={{1,0},{2,1},{3,2},{4,3},{5,4},{6,5},{7,6},{8,7},{9,8},{10,9},{11,1... | collective-permute-start | bytes 4718600 | tf_op jit(solution)/shard_map/ppermute | solution.py:17
  66.1 34.0 %collective-permute-start.2 = (bf16[24,8,2,2048]{3,1,0,2:T(8,128)(2,1)}, bf16[24,8,2,2048]{3,1,0,2:T(8,128)(2,1)}, u32[]{:S(2)}, u32[]{:S(2)}) collective-permute-start(bf16[24,8,2,2048]{3,1,0,2:T(8,128)(2,1)} %get-tuple-element.370), channel_id=1, source_target_pairs={{0,1},{1,2},{2,3},{3,4},{4,5},{5,6},{6,7},{7,8},{8,9},{9,10},{10,1... | collective-permute-start | bytes 4718600 | tf_op jit(solution)/shard_map/ppermute | solution.py:14
  69.9 885.0 %all-reduce.3.cloned.1.call-start = ((), (), s32[]{:S(2)}) async-start(), calls=%async_computation.1 | async-start | bytes 8388608
  192.6 4.6 copy-start.1
  197.6 7.6 copy-start
  205.2 452.5 %copy-start.7 = (f32[4,64,512]{2,1,0:T(8,128)S(1)}, f32[4,64,512]{2,1,0:T(8,128)}, u32[]{:S(2)}) copy-start(f32[4,64,512]{2,1,0:T(8,128)} %custom-call.3) | copy-start | bytes 1572868
  205.2 452.5 %copy-start.8 = (f32[4,64,512]{2,1,0:T(8,128)S(1)}, f32[4,64,512]{2,1,0:T(8,128)}, u32[]{:S(2)}) copy-start(f32[4,64,512]{2,1,0:T(8,128)} %custom-call.4) | copy-start | bytes 1572868
  205.2 470.0 %collective-permute-start.5 = (f32[8,32,2,2048]{3,1,0,2:T(8,128)}, f32[8,32,2,2048]{3,1,0,2:T(8,128)}, u32[]{:S(2)}, u32[]{:S(2)}) collective-permute-start(f32[8,32,2,2048]{3,1,0,2:T(8,128)} %get-tuple-element.363), channel_id=1, source_target_pairs={{16,0},{32,16},{48,32},{64,48},{80,64},{96,80},{112,96},{128,112},... | collective-permute-start | bytes 12582920 | tf_op jit(solution)/shard_map/ppermute | solution.py:25
  206.6 468.6 %collective-permute-start.4 = (f32[8,32,2,2048]{3,1,0,2:T(8,128)}, f32[8,32,2,2048]{3,1,0,2:T(8,128)}, u32[]{:S(2)}, u32[]{:S(2)}) collective-permute-start(f32[8,32,2,2048]{3,1,0,2:T(8,128)} %get-tuple-element.362), channel_id=1, source_target_pairs={{0,16},{16,32},{32,48},{48,64},{64,80},{80,96},{96,112},{112,128},... | collective-permute-start | bytes 12582920 | tf_op jit(solution)/shard_map/ppermute | solution.py:25
  681.2 1.9 copy-start.2
  683.1 10.8 %copy-start.6 = (f32[4,128,512]{1,2,0:T(8,128)S(1)}, f32[4,128,512]{1,2,0:T(8,128)}, u32[]{:S(2)}) copy-start(f32[4,128,512]{1,2,0:T(8,128)} %get-tuple-element.180) | copy-start | bytes 3145732
  684.6 271.4 %collective-permute-start.6 = (f32[8,8,2,2048]{3,1,0,2:T(8,128)}, f32[8,8,2,2048]{3,1,0,2:T(8,128)}, u32[]{:S(2)}, u32[]{:S(2)}) collective-permute-start(f32[8,8,2,2048]{3,1,0,2:T(8,128)} %get-tuple-element.369), channel_id=1, source_target_pairs={{0,1},{1,2},{2,3},{3,4},{4,5},{5,6},{6,7},{7,8},{8,9},{9,10},{10,1... | collective-permute-start | bytes 3145736 | tf_op jit(solution)/shard_map/ppermute | solution.py:25
  692.0 266.6 %collective-permute-start.7 = (f32[8,8,2,2048]{3,1,0,2:T(8,128)}, f32[8,8,2,2048]{3,1,0,2:T(8,128)}, u32[]{:S(2)}, u32[]{:S(2)}) collective-permute-start(f32[8,8,2,2048]{3,1,0,2:T(8,128)} %get-tuple-element.368), channel_id=1, source_target_pairs={{1,0},{2,1},{3,2},{4,3},{5,4},{6,5},{7,6},{8,7},{9,8},{10,9},{11,1... | collective-permute-start | bytes 3145736 | tf_op jit(solution)/shard_map/ppermute | solution.py:25
  695.0 261.0 %slice-start = ((f32[8,32,2,2048]{3,1,0,2:T(8,128)}), f32[8,16,2,2048]{3,1,0,2:T(8,128)S(1)}, s32[]{:S(2)}) async-start(f32[8,32,2,2048]{3,1,0,2:T(8,128)} %copy-done.2), calls=%async_computation.2 | async-start | bytes 4194304 | tf_op jit(solution)/shard_map/slice | solution.py:177
  954.9 2.2 copy-start.3
Sparse Core Ops, SparseCore 0:
  70.0 581.0 all-gather.1
  675.3 279.5 all-reduce.2
where the time goes:
time: 971 us; the launch traced here: 968 us
  waiting for transfers between devices  756 us (78%)
  local copies, waits for them, and re-layouts  127 us (13%)
  starting transfers between devices  31.5 us (3%)
  other arithmetic  23.2 us (2%)
  matrix products  15.9 us (2%)
  between operations  14.5 us (1%)
    all_gather x1, waiting for transfers between devices, on_device(): summary_table = lax.all_gather(summary, ('row', 'col'), axis=0, tiled=True)  437 us
    unnamed x3, waiting for transfers between devices  256 us
    ppermute x2, waiting for transfers between devices, with_halo(): lax.ppermute(lax.slice_in_dim(block, 0, width, axis=dim), axis, backward)  36.6 us
    unnamed x31, local copies, waits for them, and re-layouts  26 us
    ppermute x2, waiting for transfers between devices, with_halo(): lax.ppermute(lax.slice_in_dim(block, block.shape[dim] - width, None, axis...  25.7 us
    dynamic_slice x32, local copies, waits for them, and re-layouts, pair_grads(): lax.map(run_group, (split_heads(query_part), split_heads(grad_part), spli...  19.8 us
  transfers between devices with their start and end apart: 10, of which 5 were waited for; matrix products, arithmetic and copies ran while one was open for 16% of the time, Pallas kernels for 0%

commit v1 on v0

v1 whole, which is shorter than its diff:
```python
import math

import jax
import jax.numpy as jnp
from jax import lax
from jax.experimental import pallas as pl
from jax.experimental.pallas import tpu as pltpu
from jax.sharding import PartitionSpec as P

MESH = pl.DeviceIdType.MESH
F32 = jnp.float32
BF16 = jnp.bfloat16
LOG2E = math.log2(math.e)
SCALE = 1.0 / math.sqrt(128)
POOL = 1.0 / math.sqrt(128)
OFF = -1e30
NT = (((1,), (1,)), ((), ()))
TN = (((0,), (0,)), ((), ()))
NEAR = ((-1, 0), (1, 0), (0, -1), (0, 1), (-1, -1), (-1, 1), (1, -1), (1, 1))


def each(low, high, body):
    def step(i, carry):
        body(i)
        return carry

    lax.fori_loop(low, high, step, 0)


def pair_tile(kv, qg, norm, offset, bias):
    both = lax.dot_general(kv, qg, NT, preferred_element_type=F32)
    weights = jnp.exp2(both[:, :128] * (SCALE * LOG2E) - norm + bias)
    grads = weights * (both[:, 128:] - offset) * SCALE
    low = jnp.concatenate([grads.astype(BF16), weights.astype(BF16)], axis=1)
    grad_kv = jnp.dot(low, qg, preferred_element_type=F32)
    grad_q = lax.dot_general(low[:, :128], kv[:, :128], TN, preferred_element_type=F32)
    return grad_kv, grad_q


def kernel(
    q, k, v, go, side_in,
    gq_out, gkv_out, sg_out,
    own, side_src, side, qg, kv_land, kv, acc, gq_acc, gq_low, gkv_low,
    grad_src, grad_ud, grad_lr, win_bias, sum_bias, rows, table, tab, sum_acc, ry, rz, ry_sum, sg_src,
    ld_s, loc_s, side_ss, side_rs, in_ss, in_rs, halo_ss, halo_rs, gh_ss, gh_rs,
    za_ss, za_rs, ya_ss, ya_rs, ry_ss, ry_rs, rz_ss, rz_rs, oq_ss, oq_rs, ok_ss, ok_rs, sg_ss, sg_rs, out_s,
    from_up, from_down,
):
    row, col = lax.axis_index("row"), lax.axis_index("col")
    z, y = row // 2, col // 4
    me = lax.rem(row, 2) * 4 + lax.rem(col, 4)

    def ring(j):
        return (2 * z + j // 4, 4 * y + lax.rem(j, 4))

    def patch(dz, dy):
        return (row + 2 * dz, col + 4 * dy)

    def exists(dz, dy):
        ok = None
        for at, d, n in ((z, dz, 8), (y, dy, 4)):
            if d:
                here = (at > 0) if d < 0 else (at < n - 1)
                ok = here if ok is None else ok & here
        return ok

    def remote(src, dst, ss, rs, device):
        return pltpu.make_async_remote_copy(
            src_ref=src, dst_ref=dst, send_sem=ss, recv_sem=rs, device_id=device, device_id_type=MESH
        )

    barrier = pltpu.get_barrier_semaphore()

    def hello(device):
        pl.semaphore_signal(barrier, inc=1, device_id=device, device_id_type=MESH)

    each(1, 8, lambda o: hello(ring(lax.rem(me + o, 8))))
    each(1, 4, lambda o: hello((row, lax.rem(col + 4 * o, 16))))
    expected = jnp.int32(10)
    for dz, dy in NEAR:
        if dz:
            pl.when(exists(dz, dy))(lambda dz=dz, dy=dy: hello(patch(dz, dy)))
            expected = expected + jnp.where(exists(dz, dy), 1, 0)

    own_k = pltpu.make_async_copy(k, own.at[0], ld_s.at[0])
    own_v = pltpu.make_async_copy(v, own.at[1], ld_s.at[1])
    own_k.start()
    own_v.start()

    def local_in(s, i):
        src = (k, v, q, go)[i].at[:, pl.ds(pl.multiple_of(me * 256 + s * 128, 128), 128)]
        return pltpu.make_async_copy(src, in_dst(s, i, me), loc_s.at[s, i])

    def in_dst(s, i, slot):
        if i < 2:
            return kv_land.at[s, slot, :, pl.ds(128 * i, 128)]
        return qg.at[s, slot, pl.ds(128 * (i - 2), 128), pl.ds(128 * (i - 2), 128)]

    def d_in(s, i, o, slot):
        j = lax.rem(me + o, 8)
        src = (k, v, q, go)[i].at[:, pl.ds(pl.multiple_of(j * 256 + s * 128, 128), 128)]
        return remote(src, in_dst(s, i, slot), in_ss.at[s, i, o], in_rs.at[s, i, o], ring(j))

    for s in range(2):
        for i in range(4):
            local_in(s, i).start()

    def zero_qg(t):
        for s in range(2):
            qg[s, t, 0:128, 128:256] = jnp.zeros((128, 128), BF16)
            qg[s, t, 128:256, 0:128] = jnp.zeros((128, 128), BF16)

    each(0, 8, zero_qg)

    def zero_acc(i):
        for s in range(2):
            for b in range(4):
                acc[s, b, pl.ds(pl.multiple_of(i * 128, 128), 128), :] = jnp.zeros((128, 256), F32)

    each(0, 5, zero_acc)
    for s in range(2):
        sum_acc[s] = jnp.zeros((256, 256), F32)

    @pl.when(z == 0)
    def _():
        for s in range(2):
            kv[s, 0] = jnp.zeros((640, 256), BF16)
            grad_ud[s, 0] = jnp.zeros((640, 256), BF16)

    @pl.when(z == 7)
    def _():
        for s in range(2):
            kv[s, 3] = jnp.zeros((640, 256), BF16)
            grad_ud[s, 1] = jnp.zeros((640, 256), BF16)

    @pl.when(y == 0)
    def _():
        for s in range(2):
            for b in range(4):
                kv[s, b, 0:64] = jnp.zeros((64, 256), BF16)
            for a in range(2):
                grad_lr[s, 0, a] = jnp.zeros((64, 256), BF16)
                grad_ud[s, a, 512:576] = jnp.zeros((64, 256), BF16)

    @pl.when(y == 3)
    def _():
        for s in range(2):
            for b in range(4):
                kv[s, b, 576:640] = jnp.zeros((64, 256), BF16)
            for a in range(2):
                grad_lr[s, 1, a] = jnp.zeros((64, 256), BF16)
                grad_ud[s, a, 576:640] = jnp.zeros((64, 256), BF16)

    key_at = lax.broadcasted_iota(jnp.int32, (256, 128), 0)
    query_at = lax.broadcasted_iota(jnp.int32, (256, 128), 1)
    dc = 8 * (key_at // 64 - 1) + key_at % 8 - query_at % 16
    for j in range(3):
        dr = 8 * (j - 1) + (key_at % 64) // 8 - query_at // 16
        near = (jnp.abs(dr) <= 8) & (jnp.abs(dc) <= 8)
        win_bias[j] = jnp.where(near, F32(0), F32(OFF))

    own_k.wait()
    own_v.wait()
    for j in range(8):
        side_src[j, 0:8] = side_in[j]
        side_src[j, 8:16] = jnp.zeros((8, 128), F32)
        for i in range(2):
            total = jnp.sum(own[i, :, 256 * j : 256 * j + 256].astype(F32), axis=0, keepdims=True)
            total = (total * POOL).astype(BF16).astype(F32)
            side_src[j, 8 + i : 9 + i] = total[:, :128]
            side_src[j, 10 + i : 11 + i] = total[:, 128:]

    pl.semaphore_wait(barrier, expected)

    def d_side(o, slot):
        j = lax.rem(me + o, 8)
        return remote(side_src.at[j], side.at[slot], side_ss.at[o], side_rs.at[o], ring(j))

    each(1, 8, lambda o: d_side(o, me).start())

    def start_in(s, first):
        def body(o):
            d_in(s, first, o, me).start()
            d_in(s, first + 1, o, me).start()

        each(1, 8, body)

    def wait_in(s, first):
        def body(o):
            slot = lax.rem(me + 8 - o, 8)
            d_in(s, first, o, slot).wait_recv()
            d_in(s, first + 1, o, slot).wait_recv()

        each(1, 8, body)
        local_in(s, first).wait()
        local_in(s, first + 1).wait()

    start_in(0, 0)
    start_in(0, 2)

    def relay(_):
        @pl.when(z > 0)
        def _():
            pl.semaphore_signal(from_down, inc=1, device_id=patch(-1, 0), device_id_type=MESH)

        @pl.when(z < 7)
        def _():
            pl.semaphore_signal(from_up, inc=1, device_id=patch(1, 0), device_id_type=MESH)

        @pl.when(z > 0)
        def _():
            pl.semaphore_wait(from_up, 1)

        @pl.when(z < 7)
        def _():
            pl.semaphore_wait(from_down, 1)

    each(0, 6, relay)

    side[me] = side_src[me]
    each(1, 8, lambda o: d_side(o, lax.rem(me + 8 - o, 8)).wait_recv())
    for t in range(8):
        for s in range(2):
            for i in range(2):
                rows[8 * s + t : 8 * s + t + 1, 128 * i : 128 * i + 128] = side[t, 8 + 2 * s + i : 9 + 2 * s + i]
    table[y, z] = rows[...].astype(BF16)

    def d_za(o, slot):
        device = (lax.rem(row + 2 * o, 16), col)
        return remote(table.at[y, z], table.at[y, slot], za_ss.at[o], za_rs.at[o], device)

    each(1, 8, lambda o: d_za(o, z).start())

    def d_ya(o, slot):
        device = (row, lax.rem(col + 4 * o, 16))
        return remote(table.at[y], table.at[slot], ya_ss.at[o], ya_rs.at[o], device)

    def split(s):
        def body(t):
            block = kv_land[s, t].astype(F32).reshape(8, 16, 256)
            base = pl.multiple_of(64 + 128 * lax.rem(t, 4), 64)
            for h in range(2):
                half = block[:, 8 * h : 8 * h + 8].reshape(64, 256).astype(BF16)
                kv[s, 1 + t // 4, pl.ds(pl.multiple_of(base + 64 * h, 64), 64), :] = half

        each(0, 8, body)

    def d_halo(s, n):
        dz, dy = NEAR[n]
        bands = {-1: 1, 1: 2}.get(dz)
        to_bands = {-1: 3, 1: 0}.get(dz)
        at, to = {0: (64, 64), -1: (64, 576), 1: (512, 0)}[dy]
        size = 64 if dy else 512
        if dz:
            src, dst = kv.at[s, bands, pl.ds(at, size)], kv.at[s, to_bands, pl.ds(to, size)]
        else:
            src, dst = kv.at[s, pl.ds(1, 2), pl.ds(at, size)], kv.at[s, pl.ds(1, 2), pl.ds(to, size)]
        return remote(src, dst, halo_ss.at[s, n], halo_rs.at[s, n], patch(dz, dy))

    def start_halo(s):
        for n, (dz, dy) in enumerate(NEAR):
            pl.when(exists(dz, dy))(lambda n=n: d_halo(s, n).start())

    def wait_halo(s):
        for n, (dz, dy) in enumerate(NEAR):
            pl.when(exists(-dz, -dy))(lambda n=n: d_halo(s, n).wait_recv())

    def d_grad(s, n):
        dz, dy = NEAR[n]
        band = {-1: 0, 1: 3}.get(dz)
        at, size = {0: (64, 512), -1: (0, 64), 1: (576, 64)}[dy]
        if dz:
            src = grad_src.at[s, band, pl.ds(at, size)]
            side_at = 1 if dz < 0 else 0
            to = {0: 0, -1: 576, 1: 512}[dy]
            dst = grad_ud.at[s, side_at, pl.ds(to, size)]
        else:
            src = grad_src.at[s, pl.ds(1, 2), pl.ds(at, size)]
            dst = grad_lr.at[s, 1 if dy < 0 else 0]
        return remote(src, dst, gh_ss.at[s, n], gh_rs.at[s, n], patch(dz, dy))

    def start_grad(s):
        for band in (0, 3):
            grad_src[s, band] = acc[s, band].astype(BF16)
        for band in (1, 2):
            for at in (0, 576):
                grad_src[s, band, at : at + 64] = acc[s, band, at : at + 64].astype(BF16)
        for n, (dz, dy) in enumerate(NEAR):
            pl.when(exists(dz, dy))(lambda n=n: d_grad(s, n).start())

    def wait_grad(s):
        for n, (dz, dy) in enumerate(NEAR):
            pl.when(exists(-dz, -dy))(lambda n=n: d_grad(s, n).wait_recv())

    def window(s):
        def body(t):
            a, b = t // 4, lax.rem(t, 4)
            keys = pl.ds(pl.multiple_of(128 * b, 128), 256)
            operand = qg[s, t]
            norm, offset = side[t, s : s + 1], side[t, 2 + s : 3 + s]
            for j in range(3):
                grad_kv, grad_q = pair_tile(kv[s, a + j, keys], operand, norm, offset, win_bias[j])
                acc[s, a + j, keys] = acc[s, a + j, keys] + grad_kv
                total = grad_q if j == 0 else total + grad_q
            return total

        return body

    def summary(s):
        def body(t):
            norm, offset = side[t, s : s + 1], side[t, 2 + s : 3 + s]
            grad_kv, grad_q = pair_tile(tab[s], qg[s, t], norm, offset, sum_bias[t])
            sum_acc[s] = sum_acc[s] + grad_kv
            return grad_q

        return body

    def summary_bias(t):
        at = lax.broadcasted_iota(jnp.int32, (256, 128), 0)
        number = (2 * ((at // 8) % 8) + (at % 8) // 4) * 16 + 4 * (at // 64) + at % 4
        hit = jnp.where(number.astype(F32) == side[t, 4:5], F32(0), F32(OFF))
        sum_bias[t] = jnp.broadcast_to(jnp.max(hit, axis=1, keepdims=True), (256, 128))

    def d_ry(s, o, slot):
        to = lax.rem(y + o, 4)
        src = sum_acc.at[s, pl.ds(pl.multiple_of(64 * to, 64), 64)]
        return remote(src, ry.at[s, slot], ry_ss.at[s, o], ry_rs.at[s, o], (row, lax.rem(col + 4 * o, 16)))

    def d_rz(s, o, slot):
        to = lax.rem(z + o, 8)
        src = ry_sum.at[s, to]
        return remote(src, rz.at[s, slot], rz_ss.at[s, o], rz_rs.at[s, o], (lax.rem(row + 2 * o, 16), col))

    def start_ry(s):
        each(1, 4, lambda o: d_ry(s, o, y).start())

    def mid_reduce(s):
        each(1, 4, lambda o: d_ry(s, o, lax.rem(y + 4 - o, 4)).wait_recv())
        total = sum_acc[s, pl.ds(pl.multiple_of(64 * y, 64), 64), :]
        ry[s, y] = total
        total = (ry[s, 0] + ry[s, 1]) + (ry[s, 2] + ry[s, 3])
        ry_sum[s] = total.reshape(8, 8, 256)
        each(1, 8, lambda o: d_rz(s, o, z).start())

    def end_reduce(s):
        rz[s, z] = ry_sum[s, z]
        each(1, 8, lambda o: d_rz(s, o, lax.rem(z + 8 - o, 8)).wait_recv())
        total = rz[s, 0]
        for n in range(1, 8):
            total = total + rz[s, n]
        total = total * POOL
        for t in range(8):
            sg_src[t, s] = jnp.broadcast_to(total[t : t + 1], (8, 256))

    def d_oq(s, o, slot):
        j = lax.rem(me + o, 8)
        dst = gq_out.at[:, pl.ds(pl.multiple_of(slot * 256 + s * 128, 128), 128)]
        return remote(gq_low.at[s, j], dst, oq_ss.at[s, o], oq_rs.at[s, o], ring(j))

    def l_oq(s):
        dst = gq_out.at[:, pl.ds(pl.multiple_of(me * 256 + s * 128, 128), 128)]
        return pltpu.make_async_copy(gq_low.at[s, me], dst, out_s.at[s])

    def d_ok(s, o, slot):
        j = lax.rem(me + o, 8)
        return remote(gkv_low.at[s, j], gkv_out.at[2 * slot + s], ok_ss.at[s, o], ok_rs.at[s, o], ring(j))

    def l_ok(s):
        return pltpu.make_async_copy(gkv_low.at[s, me], gkv_out.at[2 * me + s], out_s.at[2 + s])

    def d_sg(o, slot):
        j = lax.rem(me + o, 8)
        return remote(sg_src.at[j], sg_out.at[slot], sg_ss.at[o], sg_rs.at[o], ring(j))

    l_sg = pltpu.make_async_copy(sg_src.at[me], sg_out.at[me], out_s.at[4])

    def start_oq(s):
        each(1, 8, lambda o: d_oq(s, o, me).start())
        l_oq(s).start()

    def combine(s):
        def body(t):
            a, b = t // 4, lax.rem(t, 4)
            total = acc[s, 1 + a, pl.ds(pl.multiple_of(64 + 128 * b, 64), 128), :]
            total = total + grad_ud[s, a, pl.ds(pl.multiple_of(128 * b, 128), 128), :].astype(F32)
            left = grad_lr[s, 0, a].astype(F32) + grad_ud[s, a, 512:576].astype(F32)
            right = grad_lr[s, 1, a].astype(F32) + grad_ud[s, a, 576:640].astype(F32)
            none = jnp.zeros((64, 256), F32)
            left = jnp.where(b == 0, left, none)
            right = jnp.where(b == 3, right, none)
            gkv_low[s, t] = (total + jnp.concatenate([left, right], axis=0)).astype(BF16)

        each(0, 8, body)
        each(1, 8, lambda o: d_ok(s, o, me).start())
        l_ok(s).start()

    wait_in(0, 0)
    start_in(1, 0)
    split(0)
    start_halo(0)

    each(0, 8, summary_bias)
    each(1, 8, lambda o: d_za(o, lax.rem(z + 8 - o, 8)).wait_recv())
    each(1, 4, lambda o: d_ya(o, y).start())

    wait_in(0, 2)
    start_in(1, 2)
    wait_halo(0)
    window_0 = window(0)

    def first(t):
        gq_acc[t] = window_0(t)

    each(0, 8, first)
    start_grad(0)

    each(1, 4, lambda o: d_ya(o, lax.rem(y + 4 - o, 4)).wait_recv())
    for s in range(2):
        for n in range(4):
            part = table[n].astype(F32)[:, 8 * s : 8 * s + 8]
            tab[s, 64 * n : 64 * n + 64] = part.reshape(64, 256).astype(BF16)
    summary_0 = summary(0)

    def second(t):
        gq_low[0, t] = (gq_acc[t] + summary_0(t)).astype(BF16)

    each(0, 8, second)
    start_ry(0)
    start_oq(0)

    wait_in(1, 0)
    split(1)
    start_halo(1)
    mid_reduce(0)
    wait_grad(0)
    combine(0)

    wait_in(1, 2)
    summary_1 = summary(1)

    def third(t):
        gq_acc[t] = summary_1(t)

    each(0, 8, third)
    start_ry(1)
    wait_halo(1)
    window_1 = window(1)

    def fourth(t):
        gq_low[1, t] = (gq_acc[t] + window_1(t)).astype(BF16)

    each(0, 8, fourth)
    start_grad(1)
    start_oq(1)
    mid_reduce(1)
    end_reduce(0)
    wait_grad(1)
    combine(1)
    end_reduce(1)
    each(1, 8, lambda o: d_sg(o, me).start())
    l_sg.start()

    def drain_ring(o):
        slot = lax.rem(me + 8 - o, 8)
        d_side(o, me).wait_send()
        d_za(o, z).wait_send()
        for s in range(2):
            for i in range(4):
                d_in(s, i, o, me).wait_send()
            d_rz(s, o, z).wait_send()
            d_oq(s, o, me).wait_send()
            d_oq(s, o, slot).wait_recv()
            d_ok(s, o, me).wait_send()
            d_ok(s, o, slot).wait_recv()
        d_sg(o, me).wait_send()
        d_sg(o, slot).wait_recv()

    each(1, 8, drain_ring)

    def drain_y(o):
        d_ya(o, y).wait_send()
        for s in range(2):
            d_ry(s, o, y).wait_send()

    each(1, 4, drain_y)
    for s in range(2):
        l_oq(s).wait()
        l_ok(s).wait()
        for n, (dz, dy) in enumerate(NEAR):

            def drain_near(n=n, s=s):
                d_halo(s, n).wait_send()
                d_grad(s, n).wait_send()

            pl.when(exists(dz, dy))(drain_near)
    l_sg.wait()


def finish(gq, gkv, sg, out_q, out_k, out_v):
    heads = gkv.shape[0]
    out_q[...] = gq[...].astype(F32).reshape(out_q.shape)
    for n in range(heads):
        total = gkv[n].astype(F32) + sg[n // 2, n % 2, 0:1]
        for h in range(2):
            half = total[64 * h : 64 * h + 64]
            out_k[:, 8 * h : 8 * h + 8, 128 * n : 128 * n + 128] = half[:, :128].reshape(8, 8, 128)
            out_v[:, 8 * h : 8 * h + 8, 128 * n : 128 * n + 128] = half[:, 128:].reshape(8, 8, 128)


def on_device(query_rows, key_rows, value_rows, grad_out, log_norm, grad_offset, listed):
    flat = [x.reshape(128, 2048) for x in (query_rows, key_rows, value_rows, grad_out)]
    norm = (log_norm.reshape(128, 16) * LOG2E).T.reshape(8, 2, 128)
    offset = grad_offset.reshape(128, 16).T.reshape(8, 2, 128)
    names = jnp.pad(listed.astype(F32), ((0, 0), (0, 64)), constant_values=-1.0)
    names = jnp.broadcast_to(names[None], (8, 4, 128))
    side = jnp.concatenate([norm, offset, names], axis=1)
    dma = pltpu.SemaphoreType.DMA
    gq, gkv, sg = pl.pallas_call(
        kernel,
        out_shape=(
            jax.ShapeDtypeStruct((128, 2048), BF16),
            jax.ShapeDtypeStruct((16, 128, 256), BF16),
            jax.ShapeDtypeStruct((8, 2, 8, 256), F32),
        ),
        in_specs=[pl.BlockSpec(memory_space=pl.ANY)] * 4 + [pl.BlockSpec(memory_space=pltpu.VMEM)],
        out_specs=(pl.BlockSpec(memory_space=pl.ANY),) * 3,
        scratch_shapes=[
            pltpu.VMEM((2, 128, 2048), BF16),
            pltpu.VMEM((8, 16, 128), F32),
            pltpu.VMEM((8, 16, 128), F32),
            pltpu.VMEM((2, 8, 256, 256), BF16),
            pltpu.VMEM((2, 8, 128, 256), BF16),
            pltpu.VMEM((2, 4, 640, 256), BF16),
            pltpu.VMEM((2, 4, 640, 256), F32),
            pltpu.VMEM((8, 128, 128), F32),
            pltpu.VMEM((2, 8, 128, 128), BF16),
            pltpu.VMEM((2, 8, 128, 256), BF16),
            pltpu.VMEM((2, 4, 640, 256), BF16),
            pltpu.VMEM((2, 2, 640, 256), BF16),
            pltpu.VMEM((2, 2, 2, 64, 256), BF16),
            pltpu.VMEM((3, 256, 128), F32),
            pltpu.VMEM((8, 256, 128), F32),
            pltpu.VMEM((16, 256), F32),
            pltpu.VMEM((4, 8, 16, 256), BF16),
            pltpu.VMEM((2, 256, 256), BF16),
            pltpu.VMEM((2, 256, 256), F32),
            pltpu.VMEM((2, 4, 64, 256), F32),
            pltpu.VMEM((2, 8, 8, 256), F32),
            pltpu.VMEM((2, 8, 8, 256), F32),
            pltpu.VMEM((8, 2, 8, 256), F32),
            dma((2,)), dma((2, 4)), dma((8,)), dma((8,)), dma((2, 4, 8)), dma((2, 4, 8)),
            dma((2, 8)), dma((2, 8)), dma((2, 8)), dma((2, 8)),
            dma((8,)), dma((8,)), dma((4,)), dma((4,)), dma((2, 4)), dma((2, 4)), dma((2, 8)), dma((2, 8)),
            dma((2, 8)), dma((2, 8)), dma((2, 8)), dma((2, 8)), dma((8,)), dma((8,)), dma((5,)),
            pltpu.SemaphoreType.REGULAR, pltpu.SemaphoreType.REGULAR,
        ],
        compiler_params=pltpu.CompilerParams(
            collective_id=0, has_side_effects=True, vmem_limit_bytes=48 * 2**20
        ),
        name="exchange",
    )(*flat, side)
    steps = 4
    heads = 16 // steps
    wide = heads * 128
    return pl.pallas_call(
        finish,
        grid=(steps,),
        out_shape=(jax.ShapeDtypeStruct((8, 16, 2048), F32),) * 3,
        in_specs=[
            pl.BlockSpec((128, wide), lambda i: (0, i)),
            pl.BlockSpec((heads, 128, 256), lambda i: (i, 0, 0)),
            pl.BlockSpec((heads // 2, 2, 8, 256), lambda i: (i, 0, 0, 0)),
        ],
        out_specs=(pl.BlockSpec((8, 16, wide), lambda i: (0, 0, i)),) * 3,
        compiler_params=pltpu.CompilerParams(vmem_limit_bytes=32 * 2**20),
        name="finish",
    )(gq, gkv, sg)


def solution(mesh):
    tokens = P("row", "col", None)
    return jax.shard_map(
        on_device,
        mesh=mesh,
        in_specs=(tokens,) * 6 + (P(("row", "col"), None),),
        out_specs=(tokens,) * 3,
        check_vma=False,
    )
```

time: 971 us -> 90.7 us (0.09)
  waiting for transfers between devices: 756 us -> 0 us
  local copies, waits for them, and re-layouts: 127 us -> 5.11 us
  Pallas kernels: 0 us -> 83 us
  starting transfers between devices: 31.5 us -> 0 us
  other arithmetic: 23.2 us -> 0.75 us
  matrix products: 15.9 us -> 0 us
  between operations: 14.5 us -> 0.68 us
    all_gather x1 -> x0, waiting for transfers between devices: 437 us -> none  [on_device(): summary_table = lax.all_gather(summary, ('row', 'col'), axis=0, tiled=True)]
    unnamed x3 -> x0, waiting for transfers between devices: 256 us -> none
    pallas_call x0 -> x2, Pallas kernels: none -> 83 us  [the longest x1 80.8 us: on_device(): pl.pallas_call(kernel, out_shape=(jax.ShapeDtypeStruct((128, 2048), BF16)...]
    ppermute x8 -> x0, waiting for transfers between devices: 62.3 us -> none  [the longest x2 36.6 us: with_halo(): lax.ppermute(lax.slice_in_dim(block, 0, width, axis=dim), axis, backward)]
    another operation x13 -> x0, local copies, waits for them, and re-layouts: 33.5 us -> none  [the longest x3 17.4 us: on_device(): jnp.stack([key_part.reshape(shape_window), value_part.reshape(shape_windo...]
    ppermute x8 -> x0, starting transfers between devices: 31.4 us -> none  [the longest x4 18.4 us: from_behind(): lax.ppermute(value, axis, [(source, source + steps) for source in range(f...]
    unnamed x31 -> x10, local copies, waits for them, and re-layouts: 26 us -> 4.16 us
    dynamic_slice x32 -> x0, local copies, waits for them, and re-layouts: 19.8 us -> none  [pair_grads(): lax.map(run_group, (split_heads(query_part), split_heads(grad_part), spli...]
  transfers between devices with their start and end apart: 10 -> 0, of which waited for: 5 -> 0; matrix products, arithmetic and copies ran while one was open for 16% -> 0% of each run, Pallas kernels for 0% -> 0%
where the time goes in v1:
time: 90.7 us; the launch traced here: 89.5 us
  Pallas kernels  83 us (92%)
  local copies, waits for them, and re-layouts  5.11 us (6%)
    pallas_call x1, Pallas kernels, on_device(): pl.pallas_call(kernel, out_shape=(jax.ShapeDtypeStruct((128, 2048), BF16)...  80.8 us
    unnamed x10, local copies, waits for them, and re-layouts  4.16 us
    pallas_call x1, Pallas kernels, on_device(): pl.pallas_call(finish, grid=(steps,), out_shape=(jax.ShapeDtypeStruct((8,...  2.15 us

profile of v1, /device:TPU:1, one launch (start us, length us, event | category | flops | bytes accessed | tf_op | source)
XLA Modules:
  0.0 89.5 jit_solution(2664953514697719892)
XLA Ops:
  0.6 0.0 copy-start.4
  0.6 0.7 convert_element_type.3
  1.3 0.9 copy.11
  2.2 0.0 copy-done.4
  2.3 0.1 copy.10
  2.4 0.0 copy-start
  2.4 1.0 %copy-done = bf16[8,16,2048]{2,1,0:T(8,128)(2,1)S(1)} copy-done((bf16[8,16,2048]{2,1,0:T(8,128)(2,1)S(1)}, bf16[8,16,2048]{2,1,0:T(8,128)(2,1)}, u32[]{:S(2)}) %copy-start) | copy-done | bytes 524312
  3.4 0.0 copy-start.1
  3.4 1.0 %copy-done.1 = bf16[8,16,2048]{2,1,0:T(8,128)(2,1)S(1)} copy-done((bf16[8,16,2048]{2,1,0:T(8,128)(2,1)S(1)}, bf16[8,16,2048]{2,1,0:T(8,128)(2,1)}, u32[]{:S(2)}) %copy-start.1) | copy-done | bytes 524312
  4.4 0.0 copy-start.2
  4.4 1.0 %copy-done.2 = bf16[8,16,2048]{2,1,0:T(8,128)(2,1)S(1)} copy-done((bf16[8,16,2048]{2,1,0:T(8,128)(2,1)S(1)}, bf16[8,16,2048]{2,1,0:T(8,128)(2,1)}, u32[]{:S(2)}) %copy-start.2) | copy-done | bytes 524312
  5.5 0.0 copy-start.3
  5.5 1.0 %copy-done.3 = bf16[8,16,2048]{2,1,0:T(8,128)(2,1)S(1)} copy-done((bf16[8,16,2048]{2,1,0:T(8,128)(2,1)S(1)}, bf16[8,16,2048]{2,1,0:T(8,128)(2,1)}, u32[]{:S(2)}) %copy-start.3) | copy-done | bytes 524312
  6.5 80.8 %exchange.1 = (bf16[128,2048]{1,0:T(8,128)(2,1)S(1)}, bf16[16,128,256]{2,1,0:T(8,128)(2,1)S(1)}, f32[8,2,8,256]{3,2,1,0:T(8,128)S(1)}) custom-call(bf16[128,2048]{1,0:T(8,128)(2,1)S(1)} %bitcast.14, bf16[128,2048]{1,0:T(8,128)(2,1)S(1)} %bitcast.15, bf16[128,2048]{1,0:T(8,128)(2,1)S(1)} %bitcast.16, bf16[128,2048]{1,0:T(8,128)(2,1)S(1)} %bitcast.17, ...), custom_call_target="tpu_custom_call" | custom-call | tf_op jit(solution)/shard_map/exchange/pallas_call | solution.py:518
  87.3 2.1 %finish.1 = (f32[8,16,2048]{2,1,0:T(8,128)}, f32[8,16,2048]{2,1,0:T(8,128)}, f32[8,16,2048]{2,1,0:T(8,128)}) custom-call(bf16[128,2048]{1,0:T(8,128)(2,1)S(1)} %get-tuple-element.6.gq, bf16[16,128,256]{2,1,0:T(8,128)(2,1)S(1)} %get-tuple-element.7.gkv, f32[8,2,8,256]{3,2,1,0:T(8,128)S(1)} %get-tuple-element.8.sg), custom_call_target="tpu_custom_call" | custom-call | tf_op jit(solution)/shard_map/finish/pallas_call | solution.py:565
  (4 shorter events, 0.1 us)
Async XLA Ops:
  0.6 1.6 %copy-start.4 = (f32[8,16,16]{2,1,0:T(8,128)S(1)}, f32[8,16,16]{2,1,0:T(8,128)}, u32[]{:S(2)}) copy-start(f32[8,16,16]{2,1,0:T(8,128)} %param.11) | copy-start | bytes 24580
  2.4 1.0 %copy-start = (bf16[8,16,2048]{2,1,0:T(8,128)(2,1)S(1)}, bf16[8,16,2048]{2,1,0:T(8,128)(2,1)}, u32[]{:S(2)}) copy-start(bf16[8,16,2048]{2,1,0:T(8,128)(2,1)} %param.7) | copy-start | bytes 1572868
  3.4 1.0 %copy-start.1 = (bf16[8,16,2048]{2,1,0:T(8,128)(2,1)S(1)}, bf16[8,16,2048]{2,1,0:T(8,128)(2,1)}, u32[]{:S(2)}) copy-start(bf16[8,16,2048]{2,1,0:T(8,128)(2,1)} %param.8) | copy-start | bytes 1572868
  4.4 1.0 %copy-start.2 = (bf16[8,16,2048]{2,1,0:T(8,128)(2,1)S(1)}, bf16[8,16,2048]{2,1,0:T(8,128)(2,1)}, u32[]{:S(2)}) copy-start(bf16[8,16,2048]{2,1,0:T(8,128)(2,1)} %param.9) | copy-start | bytes 1572868
  5.5 1.0 %copy-start.3 = (bf16[8,16,2048]{2,1,0:T(8,128)(2,1)S(1)}, bf16[8,16,2048]{2,1,0:T(8,128)(2,1)}, u32[]{:S(2)}) copy-start(bf16[8,16,2048]{2,1,0:T(8,128)(2,1)} %param.10) | copy-start | bytes 1572868

commit v2 on v1

v2 whole, which is shorter than its diff:
```python
import math

import jax
import jax.numpy as jnp
from jax import lax
from jax.experimental import pallas as pl
from jax.experimental.pallas import tpu as pltpu
from jax.sharding import PartitionSpec as P

MESH = pl.DeviceIdType.MESH
F32 = jnp.float32
BF16 = jnp.bfloat16
LOG2E = math.log2(math.e)
SCALE = 1.0 / math.sqrt(128)
POOL = 1.0 / math.sqrt(128)
OFF = -1e30
NT = (((1,), (1,)), ((), ()))
TN = (((0,), (0,)), ((), ()))
NEAR = ((-1, 0), (1, 0), (0, -1), (0, 1), (-1, -1), (-1, 1), (1, -1), (1, 1))


def each(low, high, body):
    def step(i, carry):
        body(i)
        return carry

    lax.fori_loop(low, high, step, 0)


def pair_tile(qg, keys, values, norm, offset, bias):
    q, go = qg[:, :128], qg[:, 128:]
    scores = lax.dot_general(q, keys, NT, preferred_element_type=F32)
    grad_weights = lax.dot_general(go, values, NT, preferred_element_type=F32)
    weights = jnp.exp2(scores * (SCALE * LOG2E) - norm + bias)
    grads = (weights * (grad_weights - offset) * SCALE).astype(BF16)
    grad_q = jnp.dot(grads, keys, preferred_element_type=F32)
    grad_k = lax.dot_general(grads, q, TN, preferred_element_type=F32)
    grad_v = lax.dot_general(weights.astype(BF16), go, TN, preferred_element_type=F32)
    return grad_k, grad_v, grad_q


def kernel(
    q, k, v, go, norm_in, offset_in, listed_in,
    gq_out, gkv_out, sg_out,
    own, own_norm, own_listed, side_src, side, side_col, qg_land, qg, kv, lanes, acc, gq_low, gkv_low,
    grad_src, grad_ud, grad_lr, win_bias, sum_bias, rows, table, tab, sum_acc, sum_low, ry, rz, ry_sum, sg_src,
    ld_s, loc_s, side_ss, side_rs, sh_ss, sh_rs, in_ss, in_rs, halo_ss, halo_rs, gh_ss, gh_rs,
    za_ss, za_rs, ya_ss, ya_rs, ry_ss, ry_rs, rz_ss, rz_rs, oq_ss, oq_rs, ok_ss, ok_rs, sg_ss, sg_rs, out_s,
    from_up, from_down,
):
    row, col = lax.axis_index("row"), lax.axis_index("col")
    z, y = row // 2, col // 4
    me = lax.rem(row, 2) * 4 + lax.rem(col, 4)

    def ring(j):
        return (2 * z + j // 4, 4 * y + lax.rem(j, 4))

    def patch(dz, dy):
        return (row + 2 * dz, col + 4 * dy)

    def exists(dz, dy):
        ok = None
        for at, d, n in ((z, dz, 8), (y, dy, 4)):
            if d:
                here = (at > 0) if d < 0 else (at < n - 1)
                ok = here if ok is None else ok & here
        return ok

    def remote(src, dst, ss, rs, device):
        return pltpu.make_async_remote_copy(
            src_ref=src, dst_ref=dst, send_sem=ss, recv_sem=rs, device_id=device, device_id_type=MESH
        )

    barrier = pltpu.get_barrier_semaphore()

    def hello(device):
        pl.semaphore_signal(barrier, inc=1, device_id=device, device_id_type=MESH)

    each(1, 8, lambda o: hello(ring(lax.rem(me + o, 8))))
    each(1, 4, lambda o: hello((row, lax.rem(col + 4 * o, 16))))
    expected = jnp.int32(10)
    for dz, dy in NEAR:
        if dz:
            pl.when(exists(dz, dy))(lambda dz=dz, dy=dy: hello(patch(dz, dy)))
            expected = expected + jnp.where(exists(dz, dy), 1, 0)

    own_k = pltpu.make_async_copy(k, own.at[0], ld_s.at[0])
    own_v = pltpu.make_async_copy(v, own.at[1], ld_s.at[1])
    own_n = pltpu.make_async_copy(norm_in, own_norm.at[0], ld_s.at[2])
    own_o = pltpu.make_async_copy(offset_in, own_norm.at[1], ld_s.at[3])
    own_l = pltpu.make_async_copy(listed_in, own_listed, ld_s.at[4])
    for copy in (own_k, own_v, own_n, own_o, own_l):
        copy.start()

    def local_in(s, i):
        src = (k, v, q, go)[i].at[:, pl.ds(pl.multiple_of(me * 256 + s * 128, 128), 128)]
        return pltpu.make_async_copy(src, in_dst(s, i, me), loc_s.at[s, i])

    def in_dst(s, i, slot):
        if i < 2:
            return kv.at[s, i, slot]
        return qg_land.at[s, slot, :, pl.ds(128 * (i - 2), 128)]

    def d_in(s, i, o, slot):
        j = lax.rem(me + o, 8)
        src = (k, v, q, go)[i].at[:, pl.ds(pl.multiple_of(j * 256 + s * 128, 128), 128)]
        return remote(src, in_dst(s, i, slot), in_ss.at[s, i, o], in_rs.at[s, i, o], ring(j))

    for s in range(2):
        for i in range(4):
            local_in(s, i).start()

    def zero_acc(i):
        for s in range(2):
            for b in range(4):
                acc[s, b, pl.ds(pl.multiple_of(i * 128, 128), 128), :] = jnp.zeros((128, 128), F32)

    each(0, 5, zero_acc)

    for at, end, band, ud in ((z, 0, 0, 0), (z, 7, 3, 1)):

        @pl.when(at == end)
        def _(band=band, ud=ud):
            for b in range(6):
                side[band, b] = jnp.zeros((16, 128), F32)
            for s in range(2):
                qg[s, band] = jnp.zeros((640, 256), BF16)
                grad_ud[s, ud] = jnp.zeros((640, 128), BF16)

    for at, end, first, block, lr, ud in ((y, 0, 0, 0, 0, 512), (y, 3, 576, 5, 1, 576)):

        @pl.when(at == end)
        def _(first=first, block=block, lr=lr, ud=ud):
            for b in range(4):
                side[b, block] = jnp.zeros((16, 128), F32)
            for s in range(2):
                for b in range(4):
                    qg[s, b, first : first + 64] = jnp.zeros((64, 256), BF16)
                for a in range(2):
                    grad_lr[s, lr, a] = jnp.zeros((64, 128), BF16)
                    grad_ud[s, a, ud : ud + 64] = jnp.zeros((64, 128), BF16)

    query_at = lax.broadcasted_iota(jnp.int32, (256, 128), 0)
    key_at = lax.broadcasted_iota(jnp.int32, (256, 128), 1)
    dc = 8 * (query_at // 64 - 1) + query_at % 8 - key_at % 16
    for j in range(3):
        dr = 8 * (j - 1) + (query_at % 64) // 8 - key_at // 16
        near = (jnp.abs(dr) <= 8) & (jnp.abs(dc) <= 8)
        win_bias[j] = jnp.where(near, F32(0), F32(OFF))

    for copy in (own_k, own_v, own_n, own_o, own_l):
        copy.wait()
    norm = own_norm[0].T * LOG2E
    offset = own_norm[1].T
    for j in range(8):
        side_src[j] = jnp.zeros((16, 128), F32)
        side_src[j, 0:2] = norm[2 * j : 2 * j + 2]
        side_src[j, 2:4] = offset[2 * j : 2 * j + 2]
        side_src[j, 4:5, 0:64] = own_listed[...].astype(F32)
        for i in range(2):
            total = jnp.sum(own[i, :, 256 * j : 256 * j + 256].astype(F32), axis=0, keepdims=True)
            total = (total * POOL).astype(BF16).astype(F32)
            side_src[j, 8 + i : 9 + i] = total[:, :128]
            side_src[j, 10 + i : 11 + i] = total[:, 128:]

    pl.semaphore_wait(barrier, expected)

    def d_side(o, slot):
        j = lax.rem(me + o, 8)
        dst = side.at[1 + slot // 4, 1 + lax.rem(slot, 4)]
        return remote(side_src.at[j], dst, side_ss.at[o], side_rs.at[o], ring(j))

    each(1, 8, lambda o: d_side(o, me).start())

    def start_in(s, first):
        def body(o):
            d_in(s, first, o, me).start()
            d_in(s, first + 1, o, me).start()

        each(1, 8, body)

    def wait_in(s, first):
        def body(o):
            slot = lax.rem(me + 8 - o, 8)
            d_in(s, first, o, slot).wait_recv()
            d_in(s, first + 1, o, slot).wait_recv()

        each(1, 8, body)
        local_in(s, first).wait()
        local_in(s, first + 1).wait()


    batches = [(0, 2), (1, 2), (0, 0), (1, 0)]
    for n in range(6):

        @pl.when(z > 0)
        def _():
            pl.semaphore_signal(from_down, inc=1, device_id=patch(-1, 0), device_id_type=MESH)

        @pl.when(z < 7)
        def _():
            pl.semaphore_signal(from_up, inc=1, device_id=patch(1, 0), device_id_type=MESH)

        if n < 4:
            start_in(*batches[n])

        @pl.when(z > 0)
        def _():
            pl.semaphore_wait(from_up, 1)

        @pl.when(z < 7)
        def _():
            pl.semaphore_wait(from_down, 1)

    side[1 + me // 4, 1 + lax.rem(me, 4)] = side_src[me]
    each(1, 8, lambda o: d_side(o, lax.rem(me + 8 - o, 8)).wait_recv())
    for t in range(8):
        for s in range(2):
            for i in range(2):
                one = side[1 + t // 4, 1 + t % 4, 8 + 2 * s + i : 9 + 2 * s + i]
                rows[8 * s + t : 8 * s + t + 1, 128 * i : 128 * i + 128] = one
    table[y, z] = rows[...].astype(BF16)

    def d_za(o, slot):
        device = (lax.rem(row + 2 * o, 16), col)
        return remote(table.at[y, z], table.at[y, slot], za_ss.at[o], za_rs.at[o], device)

    each(1, 8, lambda o: d_za(o, z).start())

    def d_ya(o, slot):
        device = (row, lax.rem(col + 4 * o, 16))
        return remote(table.at[y], table.at[slot], ya_ss.at[o], ya_rs.at[o], device)

    def split(s):
        def body(t):
            block = qg_land[s, t].astype(F32).reshape(8, 16, 256)
            base = pl.multiple_of(64 + 128 * lax.rem(t, 4), 64)
            for h in range(2):
                half = block[:, 8 * h : 8 * h + 8].reshape(64, 256).astype(BF16)
                qg[s, 1 + t // 4, pl.ds(pl.multiple_of(base + 64 * h, 64), 64), :] = half

        each(0, 8, body)

    def d_halo(s, n):
        dz, dy = NEAR[n]
        band, to_band = {-1: 1, 1: 2}.get(dz), {-1: 3, 1: 0}.get(dz)
        at, to = {0: (64, 64), -1: (64, 576), 1: (512, 0)}[dy]
        size = 64 if dy else 512
        if dz:
            src, dst = qg.at[s, band, pl.ds(at, size)], qg.at[s, to_band, pl.ds(to, size)]
        else:
            src, dst = qg.at[s, pl.ds(1, 2), pl.ds(at, size)], qg.at[s, pl.ds(1, 2), pl.ds(to, size)]
        return remote(src, dst, halo_ss.at[s, n], halo_rs.at[s, n], patch(dz, dy))

    def d_sh(n):
        dz, dy = NEAR[n]
        band, to_band = {-1: 1, 1: 2}.get(dz), {-1: 3, 1: 0}.get(dz)
        at, to = {0: (1, 1), -1: (1, 5), 1: (4, 0)}[dy]
        size = 1 if dy else 4
        if dz:
            src, dst = side.at[band, pl.ds(at, size)], side.at[to_band, pl.ds(to, size)]
        else:
            src, dst = side.at[pl.ds(1, 2), pl.ds(at, size)], side.at[pl.ds(1, 2), pl.ds(to, size)]
        return remote(src, dst, sh_ss.at[n], sh_rs.at[n], patch(dz, dy))

    def start_near(make):
        for n, (dz, dy) in enumerate(NEAR):
            pl.when(exists(dz, dy))(lambda n=n: make(n).start())

    def wait_near(make):
        for n, (dz, dy) in enumerate(NEAR):
            pl.when(exists(-dz, -dy))(lambda n=n: make(n).wait_recv())

    def spread(band, block, halves):
        columns = side[band, block].T
        side_col[...] = columns
        for s in range(2):
            for i in range(2):
                wide = jnp.broadcast_to(columns[:, 2 * i + s : 2 * i + s + 1], (128, 128)).reshape(8, 16, 128)
                for h, at in halves:
                    lanes[s, i, band, pl.ds(at, 64), :] = wide[:, 8 * h : 8 * h + 8].reshape(64, 128)

    def spread_own(t):
        band, block = 1 + t // 4, 1 + lax.rem(t, 4)
        base = 128 * block - 64
        spread(band, block, ((0, pl.multiple_of(base, 64)), (1, pl.multiple_of(base + 64, 64))))
        at = lax.broadcasted_iota(jnp.int32, (64, 256), 1)
        number = (2 * ((at // 8) % 8) + (at % 8) // 4) * 16 + 4 * (at // 64) + at % 4
        hit = jnp.where(number.astype(F32) == side_col[0:64, 4:5], F32(0), F32(OFF))
        sum_bias[t] = jnp.broadcast_to(jnp.max(hit, axis=0, keepdims=True), (8, 256))

    def spread_halo():
        for band in (0, 3):

            def middle(n, band=band):
                base = 128 * n - 64
                spread(band, n, ((0, pl.multiple_of(base, 64)), (1, pl.multiple_of(base + 64, 64))))

            each(1, 5, middle)

        def edges(band):
            spread(band, 0, ((1, 0),))
            spread(band, 5, ((0, 576),))

        each(0, 4, edges)

    def d_grad(s, n):
        dz, dy = NEAR[n]
        band = {-1: 0, 1: 3}.get(dz)
        at, size = {0: (64, 512), -1: (0, 64), 1: (576, 64)}[dy]
        if dz:
            src = grad_src.at[s, band, pl.ds(at, size)]
            side_at = 1 if dz < 0 else 0
            to = {0: 0, -1: 576, 1: 512}[dy]
            dst = grad_ud.at[s, side_at, pl.ds(to, size)]
        else:
            src = grad_src.at[s, pl.ds(1, 2), pl.ds(at, size)]
            dst = grad_lr.at[s, 1 if dy < 0 else 0]
        return remote(src, dst, gh_ss.at[s, n], gh_rs.at[s, n], patch(dz, dy))

    def start_grad(s):
        for band in (0, 3):
            grad_src[s, band] = acc[s, band].astype(BF16)
        for band in (1, 2):
            for at in (0, 576):
                grad_src[s, band, at : at + 64] = acc[s, band, at : at + 64].astype(BF16)
        start_near(lambda n: d_grad(s, n))

    def compute(s):
        def body(t, carry):
            a, b = t // 4, lax.rem(t, 4)
            queries = pl.ds(pl.multiple_of(128 * b, 128), 256)
            operand = jnp.concatenate([qg[s, a + j, queries] for j in range(3)], axis=0)
            norm = jnp.concatenate([lanes[s, 0, a + j, queries] for j in range(3)], axis=0)
            offset = jnp.concatenate([lanes[s, 1, a + j, queries] for j in range(3)], axis=0)
            bias = jnp.concatenate([win_bias[j] for j in range(3)], axis=0)
            grad_k, grad_v, grad_q = pair_tile(operand, kv[s, 0, t], kv[s, 1, t], norm, offset, bias)
            for j in range(3):
                acc[s, a + j, queries] = acc[s, a + j, queries] + grad_q[256 * j : 256 * j + 256]
            gkv_low[s, t, :, 0:128] = grad_k.astype(BF16)
            gkv_low[s, t, :, 128:256] = grad_v.astype(BF16)
            return carry

        lax.fori_loop(0, 8, body, 0, unroll=4)

    def summary(s):
        keys, values = tab[s, :, 0:128], tab[s, :, 128:256]
        for a in range(2):
            operand = qg[s, 1 + a, 64:576]
            norm, offset = lanes[s, 0, 1 + a, 64:576], lanes[s, 1, 1 + a, 64:576]
            bias = jnp.concatenate(
                [jnp.broadcast_to(sum_bias[4 * a + b, 0:1], (128, 256)) for b in range(4)], axis=0
            )
            grad_k, grad_v, grad_q = pair_tile(
                operand,
                keys,
                values,
                jnp.concatenate([norm, norm], axis=1),
                jnp.concatenate([offset, offset], axis=1),
                bias,
            )
            acc[s, 1 + a, 64:576] = acc[s, 1 + a, 64:576] + grad_q
            sum_acc[s, :, 0:128] = grad_k if a == 0 else sum_acc[s, :, 0:128] + grad_k
            sum_acc[s, :, 128:256] = grad_v if a == 0 else sum_acc[s, :, 128:256] + grad_v

    def d_ry(s, o, slot):
        to = lax.rem(y + o, 4)
        src = sum_low.at[s, pl.ds(pl.multiple_of(64 * to, 64), 64)]
        return remote(src, ry.at[s, slot], ry_ss.at[s, o], ry_rs.at[s, o], (row, lax.rem(col + 4 * o, 16)))

    def d_rz(s, o, slot):
        to = lax.rem(z + o, 8)
        src = ry_sum.at[s, to]
        return remote(src, rz.at[s, slot], rz_ss.at[s, o], rz_rs.at[s, o], (lax.rem(row + 2 * o, 16), col))

    def start_ry(s):
        sum_low[s] = sum_acc[s].astype(BF16)
        each(1, 4, lambda o: d_ry(s, o, y).start())

    def mid_reduce(s):
        each(1, 4, lambda o: d_ry(s, o, lax.rem(y + 4 - o, 4)).wait_recv())
        total = sum_acc[s, pl.ds(pl.multiple_of(64 * y, 64), 64), :]
        ry[s, y] = jnp.zeros((64, 256), BF16)
        for n in range(4):
            total = total + ry[s, n].astype(F32)
        ry_sum[s] = total.reshape(8, 8, 256)
        each(1, 8, lambda o: d_rz(s, o, z).start())

    def end_reduce(s):
        rz[s, z] = ry_sum[s, z]
        each(1, 8, lambda o: d_rz(s, o, lax.rem(z + 8 - o, 8)).wait_recv())
        total = rz[s, 0]
        for n in range(1, 8):
            total = total + rz[s, n]
        total = total * POOL
        for t in range(8):
            sg_src[t, s] = jnp.broadcast_to(total[t : t + 1], (8, 256))

    def d_oq(s, o, slot):
        j = lax.rem(me + o, 8)
        return remote(gq_low.at[s, j], gq_out.at[2 * slot + s], oq_ss.at[s, o], oq_rs.at[s, o], ring(j))

    def l_oq(s):
        return pltpu.make_async_copy(gq_low.at[s, me], gq_out.at[2 * me + s], out_s.at[s])

    def d_ok(s, o, slot):
        j = lax.rem(me + o, 8)
        return remote(gkv_low.at[s, j], gkv_out.at[2 * slot + s], ok_ss.at[s, o], ok_rs.at[s, o], ring(j))

    def l_ok(s):
        return pltpu.make_async_copy(gkv_low.at[s, me], gkv_out.at[2 * me + s], out_s.at[2 + s])

    def d_sg(o, slot):
        j = lax.rem(me + o, 8)
        return remote(sg_src.at[j], sg_out.at[slot], sg_ss.at[o], sg_rs.at[o], ring(j))

    l_sg = pltpu.make_async_copy(sg_src.at[me], sg_out.at[me], out_s.at[4])

    def start_ok(s):
        each(1, 8, lambda o: d_ok(s, o, me).start())
        l_ok(s).start()

    def combine(s):
        def body(t):
            a, b = t // 4, lax.rem(t, 4)
            total = acc[s, 1 + a, pl.ds(pl.multiple_of(64 + 128 * b, 64), 128), :]
            total = total + grad_ud[s, a, pl.ds(pl.multiple_of(128 * b, 128), 128), :].astype(F32)
            left = grad_lr[s, 0, a].astype(F32) + grad_ud[s, a, 512:576].astype(F32)
            right = grad_lr[s, 1, a].astype(F32) + grad_ud[s, a, 576:640].astype(F32)
            none = jnp.zeros((64, 128), F32)
            left = jnp.where(b == 0, left, none)
            right = jnp.where(b == 3, right, none)
            gq_low[s, t] = (total + jnp.concatenate([left, right], axis=0)).astype(BF16)

        each(0, 8, body)
        each(1, 8, lambda o: d_oq(s, o, me).start())
        l_oq(s).start()

    start_near(d_sh)
    for s in range(2):
        wait_in(s, 2)
        split(s)
        start_near(lambda n, s=s: d_halo(s, n))

    each(0, 8, spread_own)
    each(1, 8, lambda o: d_za(o, lax.rem(z + 8 - o, 8)).wait_recv())
    each(1, 4, lambda o: d_ya(o, y).start())
    wait_near(d_sh)
    spread_halo()
    wait_in(0, 0)
    wait_near(lambda n: d_halo(0, n))
    compute(0)
    start_ok(0)
    start_grad(0)
    each(1, 4, lambda o: d_ya(o, lax.rem(y + 4 - o, 4)).wait_recv())
    for s in range(2):
        for n in range(4):
            part = table[n].astype(F32)[:, 8 * s : 8 * s + 8]
            tab[s, 64 * n : 64 * n + 64] = part.reshape(64, 256).astype(BF16)
    for s in range(2):
        summary(s)
        start_ry(s)
    wait_in(1, 0)
    wait_near(lambda n: d_halo(1, n))
    compute(1)
    start_ok(1)
    start_grad(1)
    mid_reduce(0)
    mid_reduce(1)
    for s in range(2):
        wait_near(lambda n, s=s: d_grad(s, n))
        combine(s)
    end_reduce(0)
    end_reduce(1)
    each(1, 8, lambda o: d_sg(o, me).start())
    l_sg.start()

    def drain_ring(o):
        slot = lax.rem(me + 8 - o, 8)
        d_side(o, me).wait_send()
        d_za(o, z).wait_send()
        for s in range(2):
            for i in range(4):
                d_in(s, i, o, me).wait_send()
            d_rz(s, o, z).wait_send()
            d_oq(s, o, me).wait_send()
            d_oq(s, o, slot).wait_recv()
            d_ok(s, o, me).wait_send()
            d_ok(s, o, slot).wait_recv()
        d_sg(o, me).wait_send()
        d_sg(o, slot).wait_recv()

    each(1, 8, drain_ring)

    def drain_y(o):
        d_ya(o, y).wait_send()
        for s in range(2):
            d_ry(s, o, y).wait_send()

    each(1, 4, drain_y)
    for s in range(2):
        l_oq(s).wait()
        l_ok(s).wait()
        for n, (dz, dy) in enumerate(NEAR):

            def drain_near(n=n, s=s):
                d_halo(s, n).wait_send()
                d_grad(s, n).wait_send()
                if s == 0:
                    d_sh(n).wait_send()

            pl.when(exists(dz, dy))(drain_near)
    l_sg.wait()


def finish(gq, gkv, sg, out_q, out_k, out_v):
    heads = gkv.shape[0]
    for n in range(heads):
        total = gkv[n].astype(F32) + sg[n // 2, n % 2, 0:1]
        at = slice(128 * n, 128 * n + 128)
        out_k[:, :, at] = total[:, :128].reshape(8, 16, 128)
        out_v[:, :, at] = total[:, 128:].reshape(8, 16, 128)
        for h in range(2):
            out_q[:, 8 * h : 8 * h + 8, at] = gq[n, 64 * h : 64 * h + 64].astype(F32).reshape(8, 8, 128)


def on_device(query_rows, key_rows, value_rows, grad_out, log_norm, grad_offset, listed):
    flat = [x.reshape(128, 2048) for x in (query_rows, key_rows, value_rows, grad_out)]
    flat += [log_norm.reshape(128, 16), grad_offset.reshape(128, 16), listed]
    dma = pltpu.SemaphoreType.DMA
    gq, gkv, sg = pl.pallas_call(
        kernel,
        out_shape=(
            jax.ShapeDtypeStruct((16, 128, 128), BF16),
            jax.ShapeDtypeStruct((16, 128, 256), BF16),
            jax.ShapeDtypeStruct((8, 2, 8, 256), F32),
        ),
        in_specs=[pl.BlockSpec(memory_space=pltpu.HBM)] * 7,
        out_specs=(pl.BlockSpec(memory_space=pltpu.HBM),) * 3,
        scratch_shapes=[
            pltpu.VMEM((2, 128, 2048), BF16),
            pltpu.VMEM((2, 128, 16), F32),
            pltpu.VMEM((1, 64), jnp.int32),
            pltpu.VMEM((8, 16, 128), F32),
            pltpu.VMEM((4, 6, 16, 128), F32),
            pltpu.VMEM((128, 16), F32),
            pltpu.VMEM((2, 8, 128, 256), BF16),
            pltpu.VMEM((2, 4, 640, 256), BF16),
            pltpu.VMEM((2, 2, 8, 128, 128), BF16),
            pltpu.VMEM((2, 2, 4, 640, 128), F32),
            pltpu.VMEM((2, 4, 640, 128), F32),
            pltpu.VMEM((2, 8, 128, 128), BF16),
            pltpu.VMEM((2, 8, 128, 256), BF16),
            pltpu.VMEM((2, 4, 640, 128), BF16),
            pltpu.VMEM((2, 2, 640, 128), BF16),
            pltpu.VMEM((2, 2, 2, 64, 128), BF16),
            pltpu.VMEM((3, 256, 128), F32),
            pltpu.VMEM((8, 8, 256), F32),
            pltpu.VMEM((16, 256), F32),
            pltpu.VMEM((4, 8, 16, 256), BF16),
            pltpu.VMEM((2, 256, 256), BF16),
            pltpu.VMEM((2, 256, 256), F32),
            pltpu.VMEM((2, 256, 256), BF16),
            pltpu.VMEM((2, 4, 64, 256), BF16),
            pltpu.VMEM((2, 8, 8, 256), F32),
            pltpu.VMEM((2, 8, 8, 256), F32),
            pltpu.VMEM((8, 2, 8, 256), F32),
            dma((5,)), dma((2, 4)), dma((8,)), dma((8,)), dma((8,)), dma((8,)), dma((2, 4, 8)), dma((2, 4, 8)),
            dma((2, 8)), dma((2, 8)), dma((2, 8)), dma((2, 8)),
            dma((8,)), dma((8,)), dma((4,)), dma((4,)), dma((2, 4)), dma((2, 4)), dma((2, 8)), dma((2, 8)),
            dma((2, 8)), dma((2, 8)), dma((2, 8)), dma((2, 8)), dma((8,)), dma((8,)), dma((5,)),
            pltpu.SemaphoreType.REGULAR, pltpu.SemaphoreType.REGULAR,
        ],
        compiler_params=pltpu.CompilerParams(
            collective_id=0, has_side_effects=True, vmem_limit_bytes=60 * 2**20
        ),
        name="exchange",
    )(*flat)
    steps = 4
    heads = 16 // steps
    wide = heads * 128
    return pl.pallas_call(
        finish,
        grid=(steps,),
        out_shape=(jax.ShapeDtypeStruct((8, 16, 2048), F32),) * 3,
        in_specs=[
            pl.BlockSpec((heads, 128, 128), lambda i: (i, 0, 0)),
            pl.BlockSpec((heads, 128, 256), lambda i: (i, 0, 0)),
            pl.BlockSpec((heads // 2, 2, 8, 256), lambda i: (i, 0, 0, 0)),
        ],
        out_specs=(pl.BlockSpec((8, 16, wide), lambda i: (0, 0, i)),) * 3,
        compiler_params=pltpu.CompilerParams(vmem_limit_bytes=60 * 2**20),
        name="finish",
    )(gq, gkv, sg)


def solution(mesh):
    tokens = P("row", "col", None)
    return jax.shard_map(
        on_device,
        mesh=mesh,
        in_specs=(tokens,) * 6 + (P(("row", "col"), None),),
        out_specs=(tokens,) * 3,
        check_vma=False,
    )
```

time: 90.7 us -> 61.6 us (0.68); the launches traced: 89.5 us -> 61.4 us
  Pallas kernels: 83 us -> 60.7 us
  local copies, waits for them, and re-layouts: 5.11 us -> 0 us
    pallas_call x1, Pallas kernels: 80.8 us -> 56.9 us  [on_device(): pl.pallas_call(kernel, out_shape=(jax.ShapeDtypeStruct((16, 128, 128), BF...]
    unnamed x10 -> x0, local copies, waits for them, and re-layouts: 4.16 us -> none
    pallas_call x1, Pallas kernels: 2.15 us -> 3.84 us  [on_device(): pl.pallas_call(finish, grid=(steps,), out_shape=(jax.ShapeDtypeStruct((8,...]
where the time goes in v2:
time: 61.6 us; the launch traced here: 61.4 us
  Pallas kernels  60.7 us (99%)
  between operations  0.64 us (1%)
    pallas_call x1, Pallas kernels, on_device(): pl.pallas_call(kernel, out_shape=(jax.ShapeDtypeStruct((16, 128, 128), BF...  56.9 us
    pallas_call x1, Pallas kernels, on_device(): pl.pallas_call(finish, grid=(steps,), out_shape=(jax.ShapeDtypeStruct((8,...  3.84 us

profile of v2, /device:TPU:1, one launch (start us, length us, event | category | flops | bytes accessed | tf_op | source)
XLA Modules:
  0.0 61.4 jit_solution(9327371627788611548)
XLA Ops:
  0.6 56.9 %exchange.1 = (bf16[16,128,128]{2,1,0:T(8,128)(2,1)}, bf16[16,128,256]{2,1,0:T(8,128)(2,1)}, f32[8,2,8,256]{3,2,1,0:T(8,128)}) custom-call(bf16[128,2048]{1,0:T(8,128)(2,1)} %bitcast.6, bf16[128,2048]{1,0:T(8,128)(2,1)} %bitcast.7, bf16[128,2048]{1,0:T(8,128)(2,1)} %bitcast.8, bf16[128,2048]{1,0:T(8,128)(2,1)} %bitcast.9, f32[128,16]{1,0:T(8,128)} %bitcast.10, ...), custom_call_target="tpu_custom_call" | custom-call | tf_op jit(solution)/shard_map/exchange/pallas_call | solution.py:531
  57.5 3.8 %finish.1 = (f32[8,16,2048]{2,1,0:T(8,128)}, f32[8,16,2048]{2,1,0:T(8,128)}, f32[8,16,2048]{2,1,0:T(8,128)}) custom-call(bf16[16,128,128]{2,1,0:T(8,128)(2,1)} %get-tuple-element.6.gq, bf16[16,128,256]{2,1,0:T(8,128)(2,1)} %get-tuple-element.7.gkv, f32[8,2,8,256]{3,2,1,0:T(8,128)} %get-tuple-element.8.sg), custom_call_target="tpu_custom_call" | custom-call | tf_op jit(solution)/shard_map/finish/pallas_call | solution.py:582

commit v3 on v2

--- a/solution.py
+++ b/solution.py
@@ -19,12 +19,12 @@
 NEAR = ((-1, 0), (1, 0), (0, -1), (0, 1), (-1, -1), (-1, 1), (1, -1), (1, 1))
 
 
-def each(low, high, body):
+def each(low, high, body, unroll=1):
     def step(i, carry):
         body(i)
         return carry
 
-    lax.fori_loop(low, high, step, 0)
+    lax.fori_loop(low, high, step, 0, unroll=unroll)
 
 
 def pair_tile(qg, keys, values, norm, offset, bias):
@@ -43,10 +43,10 @@
     q, k, v, go, norm_in, offset_in, listed_in,
     gq_out, gkv_out, sg_out,
     own, own_norm, own_listed, side_src, side, side_col, qg_land, qg, kv, lanes, acc, gq_low, gkv_low,
-    grad_src, grad_ud, grad_lr, win_bias, sum_bias, rows, table, tab, sum_acc, sum_low, ry, rz, ry_sum, sg_src,
+    grad_src, grad_ud, grad_lr, win_bias, sum_bias, rows, table, tab, sum_acc, sum_low, ry, rz, ry_sum, ry_low, sg_src,
     ld_s, loc_s, side_ss, side_rs, sh_ss, sh_rs, in_ss, in_rs, halo_ss, halo_rs, gh_ss, gh_rs,
     za_ss, za_rs, ya_ss, ya_rs, ry_ss, ry_rs, rz_ss, rz_rs, oq_ss, oq_rs, ok_ss, ok_rs, sg_ss, sg_rs, out_s,
-    from_up, from_down,
+    from_up, from_down, from_next,
 ):
     row, col = lax.axis_index("row"), lax.axis_index("col")
     z, y = row // 2, col // 4
@@ -79,6 +79,10 @@
     each(1, 8, lambda o: hello(ring(lax.rem(me + o, 8))))
     each(1, 4, lambda o: hello((row, lax.rem(col + 4 * o, 16))))
     expected = jnp.int32(10)
+    for dz in (-3, -2, 2, 3):
+        there = (z + dz >= 0) & (z + dz <= 7)
+        pl.when(there)(lambda dz=dz: hello(patch(dz, 0)))
+        expected = expected + jnp.where(there, 1, 0)
     for dz, dy in NEAR:
         if dz:
             pl.when(exists(dz, dy))(lambda dz=dz, dy=dy: hello(patch(dz, dy)))
@@ -190,27 +194,24 @@
         local_in(s, first + 1).wait()
 
 
-    batches = [(0, 2), (1, 2), (0, 0), (1, 0)]
-    for n in range(6):
-
-        @pl.when(z > 0)
+    def tell(when, steps, flag):
+        @pl.when(when)
         def _():
-            pl.semaphore_signal(from_down, inc=1, device_id=patch(-1, 0), device_id_type=MESH)
-
-        @pl.when(z < 7)
+            pl.semaphore_signal(flag, inc=1, device_id=patch(steps, 0), device_id_type=MESH)
+
+    def told(when, flag):
+        @pl.when(when)
         def _():
-            pl.semaphore_signal(from_up, inc=1, device_id=patch(1, 0), device_id_type=MESH)
-
-        if n < 4:
-            start_in(*batches[n])
-
-        @pl.when(z > 0)
-        def _():
-            pl.semaphore_wait(from_up, 1)
-
-        @pl.when(z < 7)
-        def _():
-            pl.semaphore_wait(from_down, 1)
+            pl.semaphore_wait(flag, 1)
+
+    tell(z >= 3, -3, from_down)
+    tell(z <= 4, 3, from_up)
+    start_in(0, 2)
+    told(z <= 4, from_down)
+    told(z >= 3, from_up)
+    tell(z == 1, -1, from_next)
+    tell(z == 6, 1, from_next)
+    told((z == 0) | (z == 7), from_next)
 
     side[1 + me // 4, 1 + lax.rem(me, 4)] = side_src[me]
     each(1, 8, lambda o: d_side(o, lax.rem(me + 8 - o, 8)).wait_recv())
@@ -226,10 +227,19 @@
         return remote(table.at[y, z], table.at[y, slot], za_ss.at[o], za_rs.at[o], device)
 
     each(1, 8, lambda o: d_za(o, z).start())
-
-    def d_ya(o, slot):
+    start_in(1, 2)
+    start_in(0, 0)
+    start_in(1, 0)
+
+    def d_ya(o, n, slot):
         device = (row, lax.rem(col + 4 * o, 16))
-        return remote(table.at[y], table.at[slot], ya_ss.at[o], ya_rs.at[o], device)
+        return remote(table.at[y, n], table.at[slot, n], ya_ss.at[o, n], ya_rs.at[o, n], device)
+
+    def forward(n):
+        for o in range(1, 4):
+            d_ya(o, n, y).start()
+
+    forward(z)
 
     def split(s):
         def body(t):
@@ -296,13 +306,13 @@
                 base = 128 * n - 64
                 spread(band, n, ((0, pl.multiple_of(base, 64)), (1, pl.multiple_of(base + 64, 64))))
 
-            each(1, 5, middle)
+            each(1, 5, middle, 4)
 
         def edges(band):
             spread(band, 0, ((1, 0),))
             spread(band, 5, ((0, 576),))
 
-        each(0, 4, edges)
+        each(0, 4, edges, 4)
 
     def d_grad(s, n):
         dz, dy = NEAR[n]
@@ -368,33 +378,38 @@
         src = sum_low.at[s, pl.ds(pl.multiple_of(64 * to, 64), 64)]
         return remote(src, ry.at[s, slot], ry_ss.at[s, o], ry_rs.at[s, o], (row, lax.rem(col + 4 * o, 16)))
 
-    def d_rz(s, o, slot):
+    def d_rz(o, slot):
         to = lax.rem(z + o, 8)
-        src = ry_sum.at[s, to]
-        return remote(src, rz.at[s, slot], rz_ss.at[s, o], rz_rs.at[s, o], (lax.rem(row + 2 * o, 16), col))
+        return remote(ry_low.at[to], rz.at[slot], rz_ss.at[o], rz_rs.at[o], (lax.rem(row + 2 * o, 16), col))
 
     def start_ry(s):
         sum_low[s] = sum_acc[s].astype(BF16)
         each(1, 4, lambda o: d_ry(s, o, y).start())
 
-    def mid_reduce(s):
-        each(1, 4, lambda o: d_ry(s, o, lax.rem(y + 4 - o, 4)).wait_recv())
-        total = sum_acc[s, pl.ds(pl.multiple_of(64 * y, 64), 64), :]
-        ry[s, y] = jnp.zeros((64, 256), BF16)
-        for n in range(4):
-            total = total + ry[s, n].astype(F32)
-        ry_sum[s] = total.reshape(8, 8, 256)
-        each(1, 8, lambda o: d_rz(s, o, z).start())
-
-    def end_reduce(s):
-        rz[s, z] = ry_sum[s, z]
-        each(1, 8, lambda o: d_rz(s, o, lax.rem(z + 8 - o, 8)).wait_recv())
-        total = rz[s, 0]
-        for n in range(1, 8):
-            total = total + rz[s, n]
+    def mid_reduce():
+        totals = []
+        for s in range(2):
+            each(1, 4, lambda o: d_ry(s, o, lax.rem(y + 4 - o, 4)).wait_recv())
+            total = sum_acc[s, pl.ds(pl.multiple_of(64 * y, 64), 64), :]
+            ry[s, y] = jnp.zeros((64, 256), BF16)
+            for n in range(4):
+                total = total + ry[s, n].astype(F32)
+            totals.append(total.reshape(8, 8, 256))
+        total = jnp.concatenate(totals, axis=1)
+        ry_sum[...] = total
+        ry_low[...] = total.astype(BF16)
+        each(1, 8, lambda o: d_rz(o, z).start())
+
+    def end_reduce():
+        rz[z] = jnp.zeros((16, 256), BF16)
+        each(1, 8, lambda o: d_rz(o, lax.rem(z + 8 - o, 8)).wait_recv())
+        total = ry_sum[z]
+        for n in range(8):
+            total = total + rz[n].astype(F32)
         total = total * POOL
-        for t in range(8):
-            sg_src[t, s] = jnp.broadcast_to(total[t : t + 1], (8, 256))
+        for s in range(2):
+            for t in range(8):
+                sg_src[t, s] = jnp.broadcast_to(total[8 * s + t : 8 * s + t + 1], (8, 256))
 
     def d_oq(s, o, slot):
         j = lax.rem(me + o, 8)
@@ -437,22 +452,29 @@
         l_oq(s).start()
 
     start_near(d_sh)
-    for s in range(2):
-        wait_in(s, 2)
-        split(s)
-        start_near(lambda n, s=s: d_halo(s, n))
-
-    each(0, 8, spread_own)
-    each(1, 8, lambda o: d_za(o, lax.rem(z + 8 - o, 8)).wait_recv())
-    each(1, 4, lambda o: d_ya(o, y).start())
+    wait_in(0, 2)
+    split(0)
+    start_near(lambda n: d_halo(0, n))
+    each(0, 8, spread_own, 4)
+    wait_in(1, 2)
+    split(1)
+    start_near(lambda n: d_halo(1, n))
     wait_near(d_sh)
     spread_halo()
+
+    def pass_on(o):
+        source = lax.rem(z + 8 - o, 8)
+        d_za(o, source).wait_recv()
+        forward(source)
+
+    each(1, 8, pass_on)
     wait_in(0, 0)
     wait_near(lambda n: d_halo(0, n))
     compute(0)
     start_ok(0)
     start_grad(0)
-    each(1, 4, lambda o: d_ya(o, lax.rem(y + 4 - o, 4)).wait_recv())
+    for o in range(1, 4):
+        each(0, 8, lambda n, o=o: d_ya(o, n, lax.rem(y + 4 - o, 4)).wait_recv())
     for s in range(2):
         for n in range(4):
             part = table[n].astype(F32)[:, 8 * s : 8 * s + 8]
@@ -460,18 +482,18 @@
     for s in range(2):
         summary(s)
         start_ry(s)
+
     wait_in(1, 0)
     wait_near(lambda n: d_halo(1, n))
     compute(1)
     start_ok(1)
     start_grad(1)
-    mid_reduce(0)
-    mid_reduce(1)
-    for s in range(2):
-        wait_near(lambda n, s=s: d_grad(s, n))
-        combine(s)
-    end_reduce(0)
-    end_reduce(1)
+    mid_reduce()
+    wait_near(lambda n: d_grad(0, n))
+    combine(0)
+    wait_near(lambda n: d_grad(1, n))
+    combine(1)
+    end_reduce()
     each(1, 8, lambda o: d_sg(o, me).start())
     l_sg.start()
 
@@ -482,18 +504,18 @@
         for s in range(2):
             for i in range(4):
                 d_in(s, i, o, me).wait_send()
-            d_rz(s, o, z).wait_send()
             d_oq(s, o, me).wait_send()
             d_oq(s, o, slot).wait_recv()
             d_ok(s, o, me).wait_send()
             d_ok(s, o, slot).wait_recv()
+        d_rz(o, z).wait_send()
         d_sg(o, me).wait_send()
         d_sg(o, slot).wait_recv()
 
     each(1, 8, drain_ring)
 
     def drain_y(o):
-        d_ya(o, y).wait_send()
+        each(0, 8, lambda n: d_ya(o, n, y).wait_send())
         for s in range(2):
             d_ry(s, o, y).wait_send()
 
@@ -562,21 +584,22 @@
             pltpu.VMEM((2, 256, 256), F32),
             pltpu.VMEM((2, 256, 256), BF16),
             pltpu.VMEM((2, 4, 64, 256), BF16),
-            pltpu.VMEM((2, 8, 8, 256), F32),
-            pltpu.VMEM((2, 8, 8, 256), F32),
+            pltpu.VMEM((8, 16, 256), BF16),
+            pltpu.VMEM((8, 16, 256), F32),
+            pltpu.VMEM((8, 16, 256), BF16),
             pltpu.VMEM((8, 2, 8, 256), F32),
             dma((5,)), dma((2, 4)), dma((8,)), dma((8,)), dma((8,)), dma((8,)), dma((2, 4, 8)), dma((2, 4, 8)),
             dma((2, 8)), dma((2, 8)), dma((2, 8)), dma((2, 8)),
-            dma((8,)), dma((8,)), dma((4,)), dma((4,)), dma((2, 4)), dma((2, 4)), dma((2, 8)), dma((2, 8)),
+            dma((8,)), dma((8,)), dma((4, 8)), dma((4, 8)), dma((2, 4)), dma((2, 4)), dma((8,)), dma((8,)),
             dma((2, 8)), dma((2, 8)), dma((2, 8)), dma((2, 8)), dma((8,)), dma((8,)), dma((5,)),
-            pltpu.SemaphoreType.REGULAR, pltpu.SemaphoreType.REGULAR,
+            pltpu.SemaphoreType.REGULAR, pltpu.SemaphoreType.REGULAR, pltpu.SemaphoreType.REGULAR,
         ],
         compiler_params=pltpu.CompilerParams(
             collective_id=0, has_side_effects=True, vmem_limit_bytes=60 * 2**20
         ),
         name="exchange",
     )(*flat)
-    steps = 4
+    steps = 2
     heads = 16 // steps
     wide = heads * 128
     return pl.pallas_call(

time: 61.6 us -> 60.2 us (0.977)
  Pallas kernels: 60.7 us -> 59.4 us
    pallas_call x1, Pallas kernels: 3.84 us -> 2.85 us  [on_device(): pl.pallas_call(finish, grid=(steps,), out_shape=(jax.ShapeDtypeStruct((8,...]
where the time goes in v3:
time: 60.2 us; the launch traced here: 60.1 us
  Pallas kernels  59.4 us (99%)
  between operations  0.64 us (1%)
    pallas_call x1, Pallas kernels, on_device(): pl.pallas_call(kernel, out_shape=(jax.ShapeDtypeStruct((16, 128, 128), BF...  56.6 us
    pallas_call x1, Pallas kernels, on_device(): pl.pallas_call(finish, grid=(steps,), out_shape=(jax.ShapeDtypeStruct((8,...  2.85 us

profile of v3, /device:TPU:1, one launch (start us, length us, event | category | flops | bytes accessed | tf_op | source)
XLA Modules:
  0.0 60.1 jit_solution(1491166052970788290)
XLA Ops:
  0.6 56.6 %exchange.1 = (bf16[16,128,128]{2,1,0:T(8,128)(2,1)}, bf16[16,128,256]{2,1,0:T(8,128)(2,1)}, f32[8,2,8,256]{3,2,1,0:T(8,128)}) custom-call(bf16[128,2048]{1,0:T(8,128)(2,1)} %bitcast.6, bf16[128,2048]{1,0:T(8,128)(2,1)} %bitcast.7, bf16[128,2048]{1,0:T(8,128)(2,1)} %bitcast.8, bf16[128,2048]{1,0:T(8,128)(2,1)} %bitcast.9, f32[128,16]{1,0:T(8,128)} %bitcast.10, ...), custom_call_target="tpu_custom_call" | custom-call | tf_op jit(solution)/shard_map/exchange/pallas_call | solution.py:553
  57.2 2.8 %finish.1 = (f32[8,16,2048]{2,1,0:T(8,128)}, f32[8,16,2048]{2,1,0:T(8,128)}, f32[8,16,2048]{2,1,0:T(8,128)}) custom-call(bf16[16,128,128]{2,1,0:T(8,128)(2,1)} %get-tuple-element.6.gq, bf16[16,128,256]{2,1,0:T(8,128)(2,1)} %get-tuple-element.7.gkv, f32[8,2,8,256]{3,2,1,0:T(8,128)} %get-tuple-element.8.sg), custom_call_target="tpu_custom_call" | custom-call | tf_op jit(solution)/shard_map/finish/pallas_call | solution.py:605

commit v4 on v3

--- a/solution.py
+++ b/solution.py
@@ -351,7 +351,7 @@
             gkv_low[s, t, :, 128:256] = grad_v.astype(BF16)
             return carry
 
-        lax.fori_loop(0, 8, body, 0, unroll=4)
+        lax.fori_loop(0, 8, body, 0, unroll=8)
 
     def summary(s):
         keys, values = tab[s, :, 0:128], tab[s, :, 128:256]
@@ -456,18 +456,18 @@
     split(0)
     start_near(lambda n: d_halo(0, n))
     each(0, 8, spread_own, 4)
+
+    def pass_on(o):
+        source = lax.rem(z + 8 - o, 8)
+        d_za(o, source).wait_recv()
+        forward(source)
+
+    each(1, 8, pass_on)
     wait_in(1, 2)
     split(1)
     start_near(lambda n: d_halo(1, n))
     wait_near(d_sh)
     spread_halo()
-
-    def pass_on(o):
-        source = lax.rem(z + 8 - o, 8)
-        d_za(o, source).wait_recv()
-        forward(source)
-
-    each(1, 8, pass_on)
     wait_in(0, 0)
     wait_near(lambda n: d_halo(0, n))
     compute(0)

time: 60.2 us -> 60.1 us (level)
  no operation moved by 1% of the time
where the time goes in v4:
time: 60.1 us; the launch traced here: 59.9 us
  Pallas kernels  59.3 us (99%)
  between operations  0.64 us (1%)
    pallas_call x1, Pallas kernels, on_device(): pl.pallas_call(kernel, out_shape=(jax.ShapeDtypeStruct((16, 128, 128), BF...  56.5 us
    pallas_call x1, Pallas kernels, on_device(): pl.pallas_call(finish, grid=(steps,), out_shape=(jax.ShapeDtypeStruct((8,...  2.85 us

profile of v4, /device:TPU:1, one launch (start us, length us, event | category | flops | bytes accessed | tf_op | source)
XLA Modules:
  0.0 59.9 jit_solution(8233878983986401219)
XLA Ops:
  0.6 56.5 %exchange.1 = (bf16[16,128,128]{2,1,0:T(8,128)(2,1)}, bf16[16,128,256]{2,1,0:T(8,128)(2,1)}, f32[8,2,8,256]{3,2,1,0:T(8,128)}) custom-call(bf16[128,2048]{1,0:T(8,128)(2,1)} %bitcast.6, bf16[128,2048]{1,0:T(8,128)(2,1)} %bitcast.7, bf16[128,2048]{1,0:T(8,128)(2,1)} %bitcast.8, bf16[128,2048]{1,0:T(8,128)(2,1)} %bitcast.9, f32[128,16]{1,0:T(8,128)} %bitcast.10, ...), custom_call_target="tpu_custom_call" | custom-call | tf_op jit(solution)/shard_map/exchange/pallas_call | solution.py:553
  57.1 2.8 %finish.1 = (f32[8,16,2048]{2,1,0:T(8,128)}, f32[8,16,2048]{2,1,0:T(8,128)}, f32[8,16,2048]{2,1,0:T(8,128)}) custom-call(bf16[16,128,128]{2,1,0:T(8,128)(2,1)} %get-tuple-element.6.gq, bf16[16,128,256]{2,1,0:T(8,128)(2,1)} %get-tuple-element.7.gkv, f32[8,2,8,256]{3,2,1,0:T(8,128)} %get-tuple-element.8.sg), custom_call_target="tpu_custom_call" | custom-call | tf_op jit(solution)/shard_map/finish/pallas_call | solution.py:605
